TPU v7x, 32 devices: a whole 2x2x4 slice. The times are simulated.
32 devices in a mesh: dp: 8 (over y, x, core), tensor: 4 (over z).
Axes of the slice: x: 2, y: 2, z: 4, core: 2. Of those that a mesh axis runs over, the one named last changes fastest.
Arguments:
- tokens: bfloat16 [8, 1032, 1024], P('dp', 'tensor'), may hold values from -6 to 6
- cotangent: bfloat16 [8, 1032, 1024], P('dp', 'tensor'), may hold values from -6 to 6
- w_qkv: bfloat16 [3, 1024, 1024], P(None, 'dp', 'tensor'), may hold values from -0.1875 to 0.1875
- w_o: bfloat16 [1024, 1024], P('tensor', 'dp'), may hold values from -0.1875 to 0.1875
- w_gu: bfloat16 [2, 1024, 2736], P(None, 'dp', 'tensor'), may hold values from -0.1875 to 0.1875
- w_down: bfloat16 [2736, 1024], P('tensor', 'dp'), may hold values from -0.109375 to 0.109375
- norm_params: float32 [6, 1024], replicated, may hold values from -1.5 to 1.65, as said below
- head_params: float32 [4, 1024], replicated, may hold values from -1.5 to 1.65, as said below
- ffn_params: float32 [4, 2736], replicated, may hold values from -1.5 to 1.65, as said below
- token_mask: int32 [8, 1032], P('dp'), may hold values from 0 to 1, as said below
- empty_flag: int32 [8], P('dp'), may hold values from 0 to 1, as said below
- coords: int32 [8, 2, 1032], P('dp'), may hold values from 0 to 31, as said below
Outputs:
- layer_out: bfloat16 [8, 1032, 1024], P('dp', 'tensor')
- d_tokens: float32 [8, 1032, 1024], P('dp', 'tensor')
- d_w_qkv: float32 [3, 1024, 1024], P(None, 'dp', 'tensor')
- d_w_o: float32 [1024, 1024], P('tensor', 'dp')
- d_w_gu: float32 [2, 1024, 2736], P(None, 'dp', 'tensor')
- d_w_down: float32 [2736, 1024], P('tensor', 'dp')
- d_norm_params: float32 [6, 1024], replicated
- d_head_params: float32 [4, 1024], replicated
- d_ffn_params: float32 [4, 2736], replicated
Inputs may be any that keep to these rules, and one draw needn't show every extreme that they name: `token_mask`: in every image slot 0 (the class token) is 1, the patch slots 1 to 1024 are 1 or 0, and the later slots are 0. `empty_flag`: at least one image is flagged. `coords`: row 0 holds grid rows, row 1 grid columns; the patch slots of an image hold every position of the 32 x 32 grid once, in an order drawn per image; slot 0 and the later slots hold 0. `norm_params`: gain rows lie within 0.6 to 1.65, the other rows within -1.5 to 1.5. `head_params`: gain rows lie within 0.6 to 1.65, the other rows within -1.5 to 1.5. `ffn_params`: gain rows lie within 0.6 to 1.65, the other rows within -1.5 to 1.5.
All inputs are finite; a program needn't handle non-finite values.
Results may differ from a plain program's by a relative error of at most 0.015.
Values may be sent and summed in bfloat16 or wider, within the bound.
No kernel may reach another device: no remote copies, remote signals or barrier semaphores. Data moves between devices by JAX's collectives and lax.ppermute only.
A program may use at most 192 MiB of HBM per device.

v0:
```python
import math

import jax
import jax.numpy as jnp
from jax import lax
from jax.sharding import PartitionSpec as P

FF = 2730
HD = 64
FF_PAD = 2736


def gather_rows(rows_in):
    return lax.all_gather(rows_in, "tensor", axis=1, tiled=True)


def scatter_rows(rows_in):
    return lax.psum_scatter(rows_in, "tensor", scatter_dimension=1, tiled=True)


def row_sums(pair_sums, is_split):
    if is_split:
        return lax.psum((pair_sums[0], pair_sums[1]), "tensor")
    return pair_sums


def norm_forward(values_in, gain_vec, shift_vec, mask_vec, unit_count, is_split):
    first_sum, second_sum = row_sums(
        (
            jnp.sum(values_in * mask_vec, axis=-1),
            jnp.sum(values_in * values_in * mask_vec, axis=-1),
        ),
        is_split,
    )
    mean_row = first_sum[..., None] / unit_count
    inv_std = lax.rsqrt(second_sum[..., None] / unit_count - mean_row * mean_row + 1e-06)
    unit_value = (values_in - mean_row) * inv_std
    return (mask_vec * (unit_value * gain_vec + shift_vec), unit_value, inv_std)


def norm_backward(d_out, gain_vec, unit_value, inv_std, mask_vec, unit_count, is_split):
    scaled = d_out * gain_vec * mask_vec
    first_sum, second_sum = row_sums(
        (jnp.sum(scaled, axis=-1), jnp.sum(scaled * unit_value, axis=-1)), is_split
    )
    d_in = (
        mask_vec
        * inv_std
        * (
            scaled
            - first_sum[..., None] / unit_count
            - unit_value * (second_sum[..., None] / unit_count)
        )
    )
    lead_axes = tuple(range(d_out.ndim - 1))
    return (
        d_in,
        jnp.sum(d_out * unit_value * mask_vec, axis=lead_axes),
        jnp.sum(d_out * mask_vec, axis=lead_axes),
    )


def rope_tables(coords):
    half_dim = HD // 2
    index_j = jnp.arange(half_dim // 2).astype(jnp.float32)
    frequency = jnp.repeat(jnp.exp(index_j * (-2.0 * math.log(10000.0) / half_dim)), 2)
    places = coords.astype(jnp.float32) * 0.5
    angles = jnp.concatenate(
        [places[:, 0, :, None] * frequency, places[:, 1, :, None] * frequency], axis=-1
    )
    return (jnp.cos(angles)[:, :, None, :], jnp.sin(angles)[:, :, None, :])


def turn_pairs(heads_in):
    pair_view = heads_in.reshape(heads_in.shape[:-1] + (heads_in.shape[-1] // 2, 2))
    return jnp.stack([-pair_view[..., 1], pair_view[..., 0]], axis=-1).reshape(heads_in.shape)


def block_rows(seq_len):
    pieces = max(1, seq_len // 512)
    while seq_len % pieces:
        pieces -= 1
    return pieces


def embed_columns(local_part, offset, full_width):
    canvas = jnp.zeros((local_part.shape[0], full_width), jnp.float32)
    return lax.dynamic_update_slice(canvas, local_part, (0, offset))


def on_device(
    tokens,
    cotangent,
    w_qkv,
    w_o,
    w_gu,
    w_down,
    norm_params,
    head_params,
    ffn_params,
    token_mask,
    empty_flag,
    coords,
):
    tp_index = lax.axis_index("tensor")
    n_images, own_rows, model_width = tokens.shape
    seq_len = token_mask.shape[1]
    local_width = w_qkv.shape[2]
    local_heads = local_width // HD
    local_units = w_gu.shape[2]
    score_scale = HD ** (-0.5)
    row_start = tp_index * own_rows
    head_offset = tp_index * local_width
    unit_offset = tp_index * local_units
    ones_vec = jnp.ones((model_width,), jnp.float32)
    valid_keys = token_mask > 0
    keep_full = token_mask.astype(jnp.float32) * (1.0 - empty_flag.astype(jnp.float32))[:, None]
    keep_rows = lax.dynamic_slice_in_dim(keep_full, row_start, own_rows, 1)[..., None]
    cosine, sine_tab = rope_tables(coords)
    head_local = lax.dynamic_slice_in_dim(head_params, head_offset, local_width, 1)
    ffn_local = lax.dynamic_slice_in_dim(ffn_params, unit_offset, local_units, 1)
    full_qkv, full_o, full_gu, full_down = (
        lax.all_gather(w_qkv, "dp", axis=1, tiled=True),
        lax.all_gather(w_o, "dp", axis=1, tiled=True),
        lax.all_gather(w_gu, "dp", axis=1, tiled=True),
        lax.all_gather(w_down, "dp", axis=1, tiled=True),
    )
    image_rows = tokens.astype(jnp.float32)
    normed_own, unit_one, inv_one = norm_forward(
        image_rows, norm_params[0], norm_params[1], ones_vec, model_width, False
    )
    normed_low = gather_rows(normed_own.astype(jnp.bfloat16))
    projected = jnp.einsum(
        "isd,cde->cise", normed_low, full_qkv, preferred_element_type=jnp.float32
    )
    heads_shape = (n_images, seq_len, local_heads, HD)
    query_pre = (projected[0] + head_local[0]).reshape(heads_shape)
    key_pre = projected[1].reshape(heads_shape)
    query_low = (query_pre * cosine + turn_pairs(query_pre) * sine_tab).astype(jnp.bfloat16)
    key_low = (key_pre * cosine + turn_pairs(key_pre) * sine_tab).astype(jnp.bfloat16)
    value_low = (projected[2] + head_local[1]).reshape(heads_shape).astype(jnp.bfloat16)
    blocks = block_rows(seq_len)
    block_len = seq_len // blocks
    per_image = local_heads * blocks
    item_count = n_images * per_image

    def locate(index_t):
        image_at = index_t // per_image
        head_at = index_t // blocks % local_heads
        start_at = index_t % blocks * block_len
        return (image_at, head_at, start_at)

    def take_heads(source, image_at, head_at, start_at, length):
        return lax.dynamic_slice(
            source, (image_at, start_at, head_at, 0), (1, length, 1, HD)
        ).reshape(length, HD)

    def block_probs(query_blk, key_all):
        valid_row = valid_keys[0]
        scores = (
            lax.dot_general(
                query_blk, key_all, (((1,), (1,)), ((), ())), preferred_element_type=jnp.float32
            )
            * score_scale
        )
        return jnp.where(valid_row[None, :], scores, -1e30)

    def attend(index_t):
        image_at, head_at, start_at = locate(index_t)
        query_blk = take_heads(query_low, image_at, head_at, start_at, block_len)
        key_all = take_heads(key_low, image_at, head_at, 0, seq_len)
        value_all = take_heads(value_low, image_at, head_at, 0, seq_len)
        scores = block_probs(query_blk, key_all)
        row_max = jnp.max(scores, axis=-1, keepdims=True)
        exp_score = jnp.exp(scores - row_max)
        row_total = jnp.sum(exp_score, axis=-1, keepdims=True)
        attn_probs = (exp_score / row_total).astype(jnp.bfloat16)
        out_blk = jnp.dot(attn_probs, value_all, preferred_element_type=jnp.float32)
        return (out_blk, (row_max + jnp.log(row_total))[:, 0])

    mixed_blocks, log_total = lax.map(attend, jnp.arange(item_count))
    mixed_heads = (
        mixed_blocks.reshape(n_images, local_heads, blocks, block_len, HD)
        .transpose(0, 2, 3, 1, 4)
        .reshape(n_images, seq_len, local_width)
    )
    mixed_rows = lax.all_to_all(mixed_heads, "tensor", split_axis=1, concat_axis=2, tiled=True)
    whole_o = lax.all_gather(full_o, "tensor", axis=0, tiled=True)
    inner_normed, unit_two, inv_two = norm_forward(
        mixed_rows, head_params[2], head_params[3], ones_vec, model_width, False
    )
    inner_low = inner_normed.astype(jnp.bfloat16)
    branch = (
        jnp.einsum("isd,de->ise", inner_low, whole_o, preferred_element_type=jnp.float32)
        + norm_params[4]
    )
    middle = image_rows + keep_rows * branch
    normed_two, unit_three, inv_three = norm_forward(
        middle, norm_params[2], norm_params[3], ones_vec, model_width, False
    )
    normed_two_low = gather_rows(normed_two.astype(jnp.bfloat16))
    gate_up = jnp.einsum(
        "isd,cdf->cisf", normed_two_low, full_gu, preferred_element_type=jnp.float32
    )
    gate_act = gate_up[0] + ffn_local[0]
    up_act = gate_up[1] + ffn_local[1]
    sigmoid_g = 1.0 / (1.0 + jnp.exp(-gate_act))
    silu_g = gate_act * sigmoid_g
    hidden = silu_g * up_act
    unit_mask = (unit_offset + jnp.arange(local_units) < FF).astype(jnp.float32)
    ffn_normed, unit_four, inv_four = norm_forward(
        hidden, ffn_local[2], ffn_local[3], unit_mask, FF, True
    )
    ffn_low = ffn_normed.astype(jnp.bfloat16)
    branch_two = (
        scatter_rows(
            jnp.einsum("isf,fe->ise", ffn_low, full_down, preferred_element_type=jnp.float32)
        )
        + norm_params[5]
    )
    layer_out = middle + keep_rows * branch_two
    d_out = cotangent.astype(jnp.float32)
    d_branch_two = (keep_rows * d_out).astype(jnp.bfloat16)
    d_rows_two = gather_rows(d_branch_two)
    d_ffn = jnp.einsum("ise,fe->isf", d_rows_two, full_down, preferred_element_type=jnp.float32)
    grad_down = jnp.einsum("isf,ise->fe", ffn_low, d_rows_two, preferred_element_type=jnp.float32)
    d_hidden, grad_ffn_gain, grad_ffn_shift = norm_backward(
        d_ffn, ffn_local[2], unit_four, inv_four, unit_mask, FF, True
    )
    d_gate = (d_hidden * up_act * sigmoid_g * (1.0 + gate_act * (1.0 - sigmoid_g))).astype(
        jnp.bfloat16
    )
    d_up = (d_hidden * silu_g).astype(jnp.bfloat16)
    d_gate_up = jnp.stack([d_gate, d_up])
    grad_gu = jnp.einsum(
        "isd,cisf->cdf", normed_two_low, d_gate_up, preferred_element_type=jnp.float32
    )
    d_normed_two = scatter_rows(
        jnp.einsum("cisf,cdf->isd", d_gate_up, full_gu, preferred_element_type=jnp.float32)
    )
    d_middle_part, grad_gain_two, grad_shift_two = norm_backward(
        d_normed_two, norm_params[2], unit_three, inv_three, ones_vec, model_width, False
    )
    d_middle = d_out + d_middle_part
    d_branch = (keep_rows * d_middle).astype(jnp.bfloat16)
    d_inner = jnp.einsum("ise,de->isd", d_branch, whole_o, preferred_element_type=jnp.float32)
    grad_o_whole = jnp.einsum(
        "isd,ise->de", inner_low, d_branch, preferred_element_type=jnp.float32
    )
    d_mixed_rows, grad_inner_gain, grad_inner_shift = norm_backward(
        d_inner, head_params[2], unit_two, inv_two, ones_vec, model_width, False
    )
    d_mixed_low = lax.all_to_all(
        d_mixed_rows.astype(jnp.bfloat16), "tensor", split_axis=2, concat_axis=1, tiled=True
    )
    grad_o = lax.psum_scatter(
        grad_o_whole.astype(jnp.bfloat16), "tensor", scatter_dimension=0, tiled=True
    )
    inner_grads = jnp.stack([grad_inner_gain, grad_inner_shift])
    d_mixed_heads = d_mixed_low.reshape(heads_shape)

    def attend_back(index_t):
        image_at, head_at, start_at = locate(index_t)
        query_blk = take_heads(query_low, image_at, head_at, start_at, block_len)
        key_all = take_heads(key_low, image_at, head_at, 0, seq_len)
        value_all = take_heads(value_low, image_at, head_at, 0, seq_len)
        d_blk = take_heads(d_mixed_heads, image_at, head_at, start_at, block_len)
        scores = block_probs(query_blk, key_all)
        attn_probs = jnp.exp(scores - log_total[index_t][:, None])
        d_probs = lax.dot_general(
            d_blk, value_all, (((1,), (1,)), ((), ())), preferred_element_type=jnp.float32
        )
        d_scores = (
            attn_probs * (d_probs - jnp.sum(attn_probs * d_probs, axis=-1, keepdims=True))
        ).astype(jnp.bfloat16)
        d_query = jnp.dot(d_scores, key_all, preferred_element_type=jnp.float32) * score_scale
        d_key = (
            lax.dot_general(
                d_scores, query_blk, (((0,), (0,)), ((), ())), preferred_element_type=jnp.float32
            )
            * score_scale
        )
        d_value = lax.dot_general(
            attn_probs.astype(jnp.bfloat16),
            d_blk,
            (((0,), (0,)), ((), ())),
            preferred_element_type=jnp.float32,
        )
        return (d_query, d_key, d_value)

    d_query_b, d_key_b, d_value_b = lax.map(attend_back, jnp.arange(item_count))
    d_query = (
        d_query_b.reshape(n_images, local_heads, blocks, block_len, HD)
        .transpose(0, 2, 3, 1, 4)
        .reshape(heads_shape)
    )
    d_key = (
        d_key_b.reshape(n_images, local_heads, blocks, seq_len, HD)
        .sum(axis=2)
        .transpose(0, 2, 1, 3)
    )
    d_value = (
        d_value_b.reshape(n_images, local_heads, blocks, seq_len, HD)
        .sum(axis=2)
        .transpose(0, 2, 1, 3)
    )
    flat_shape = (n_images, seq_len, local_width)
    d_query_pre = (
        (d_query * cosine - turn_pairs(d_query) * sine_tab).reshape(flat_shape).astype(jnp.bfloat16)
    )
    d_key_pre = (
        (d_key * cosine - turn_pairs(d_key) * sine_tab).reshape(flat_shape).astype(jnp.bfloat16)
    )
    d_value_pre = d_value.reshape(flat_shape).astype(jnp.bfloat16)
    d_proj = jnp.stack([d_query_pre, d_key_pre, d_value_pre])
    grad_qkv = jnp.einsum("isd,cise->cde", normed_low, d_proj, preferred_element_type=jnp.float32)
    d_normed = scatter_rows(
        jnp.einsum("cise,cde->isd", d_proj, full_qkv, preferred_element_type=jnp.float32)
    )
    d_input_part, grad_gain_one, grad_shift_one = norm_backward(
        d_normed, norm_params[0], unit_one, inv_one, ones_vec, model_width, False
    )
    d_tokens = d_middle + d_input_part
    norm_grads = jnp.stack(
        [
            grad_gain_one,
            grad_shift_one,
            grad_gain_two,
            grad_shift_two,
            jnp.sum(d_branch.astype(jnp.float32), axis=(0, 1)),
            jnp.sum(d_branch_two.astype(jnp.float32), axis=(0, 1)),
        ]
    )
    bias_grads = jnp.stack(
        [
            jnp.sum(d_query_pre.astype(jnp.float32), axis=(0, 1)),
            jnp.sum(d_value_pre.astype(jnp.float32), axis=(0, 1)),
        ]
    )
    head_grads = jnp.concatenate(
        [embed_columns(bias_grads, head_offset, model_width), inner_grads], axis=0
    )
    ffn_grads = embed_columns(
        jnp.stack(
            [
                jnp.sum(d_gate.astype(jnp.float32), axis=(0, 1)),
                jnp.sum(d_up.astype(jnp.float32), axis=(0, 1)),
                grad_ffn_gain,
                grad_ffn_shift,
            ]
        ),
        unit_offset,
        FF_PAD,
    )
    norm_total, head_total, ffn_total = lax.psum(
        (norm_grads, head_grads, ffn_grads), ("dp", "tensor")
    )
    grad_qkv_own, grad_o_own, grad_gu_own, grad_down_own = (
        lax.psum_scatter(
            grad_qkv.astype(jnp.bfloat16), "dp", scatter_dimension=1, tiled=True
        ).astype(jnp.float32),
        lax.psum_scatter(grad_o, "dp", scatter_dimension=1, tiled=True).astype(jnp.float32),
        lax.psum_scatter(
            grad_gu.astype(jnp.bfloat16), "dp", scatter_dimension=1, tiled=True
        ).astype(jnp.float32),
        lax.psum_scatter(
            grad_down.astype(jnp.bfloat16), "dp", scatter_dimension=1, tiled=True
        ).astype(jnp.float32),
    )
    return (
        layer_out.astype(jnp.bfloat16),
        d_tokens,
        grad_qkv_own,
        grad_o_own,
        grad_gu_own,
        grad_down_own,
        norm_total,
        head_total,
        ffn_total,
    )


def solution(mesh):
    placed = (
        P("dp", "tensor", None),
        P("dp", "tensor", None),
        P(None, "dp", "tensor"),
        P("tensor", "dp"),
        P(None, "dp", "tensor"),
        P("tensor", "dp"),
        P(),
        P(),
        P(),
        P("dp", None),
        P("dp"),
        P("dp", None, None),
    )
    return jax.shard_map(
        on_device,
        mesh=mesh,
        in_specs=placed,
        out_specs=(
            P("dp", "tensor", None),
            P("dp", "tensor", None),
            P(None, "dp", "tensor"),
            P("tensor", "dp"),
            P(None, "dp", "tensor"),
            P("tensor", "dp"),
            P(),
            P(),
            P(),
        ),
        check_vma=False,
    )
```

profile of v0, /device:TPU:0, one launch (start us, length us, event | category | flops | bytes accessed | tf_op | source)
XLA Modules:
  0.0 1423.0 jit_solution(10229722797825496752)
XLA Ops:
  14.7 13.0 all_gather.26
  32.4 7.0 all-gather.10.cloned.1.call-done
  39.4 83.5 %all-gather.8.cloned.1.call-done = bf16[1,1032,1024]{2,0,1:T(2,128)(2,1)} async-done(((bf16[1,258,1024]{2,0,1:T(2,128)(2,1)}), bf16[1,1032,1024]{2,0,1:T(2,128)(2,1)}) %all-gather.8.cloned.1.call-update) | async-done | bytes 2113552 | tf_op jit(solution)/shard_map/all_gather | solution.py:14
  122.9 4.6 convolution_bitcast_fusion.5
  153.5 73.9 %while.32 = (s32[]{:T(128)}, f32[8,516,64]{1,2,0:T(8,128)}, f32[8,516]{1,0:T(8,128)}, pred[1,1032]{1,0:T(4,128)(4,1)S(1)}, s32[8]{0:T(128)S(1)}, /*index=5*/bf16...) while((s32[]{:T(128)}, f32[8,516,64]{1,2,0:T(8,128)}, ...), condition=%wide.region_5.6_spmd, body=%wide.region_2.5_spmd.sunk | while | flops 140582688 | bytes 6962298 | solution.py:181
  239.8 25.4 %all-to-all-done = f32[1,1032,256]{2,0,1:T(1,128)S(1)} async-done(((f32[1,1032,256]{2,0,1:T(1,128)}), f32[1,1032,256]{2,0,1:T(1,128)S(1)}, u32[]{:S(2)}, u32[]{:S(2)}) %all-to-all-start) | async-done | bytes 1056800 | tf_op jit(solution)/shard_map/all_to_all | solution.py:187
  265.2 7.8 fusion.123
  284.2 76.8 %all-gather.14.cloned.1.call-done = bf16[1,1032,1024]{2,0,1:T(2,128)(2,1)} async-done(((bf16[1,258,1024]{2,0,1:T(2,128)(2,1)}), bf16[1,1032,1024]{2,0,1:T(2,128)(2,1)}) %all-gather.14.cloned.1.call-update) | async-done | bytes 2113552 | tf_op jit(solution)/shard_map/all_gather | solution.py:14
  361.0 7.0 convolution_bitcast_fusion.1
  370.7 9.3 all-reduce.5
  380.1 6.4 all-gather.18.cloned.1.call-done
  386.5 82.9 %all-gather.20.cloned.1.call-done = bf16[1,1032,1024]{2,0,1:T(2,128)(2,1)} async-done(((bf16[1,258,1024]{2,0,1:T(2,128)(2,1)}), bf16[1,1032,1024]{2,0,1:T(2,128)(2,1)}) %all-gather.20.cloned.1.call-update) | async-done | bytes 2113552 | tf_op jit(solution)/shard_map/all_gather | solution.py:14
  469.4 11.3 multiply_reduce_fusion.2
  480.6 9.3 all-reduce.4
  490.0 6.5 convert_reduce_fusion.1
  500.1 8.4 copy.187
  511.2 152.6 %all-reduce.11.cloned.1.call-done = f32[1,1032,1024]{2,0,1:T(1,128)} async-done(((f32[1,1032,1024]{2,0,1:T(1,128)}), f32[1,1032,1024]{2,0,1:T(1,128)}) %all-reduce.11.cloned.1.call-update) | async-done | bytes 4227088
  672.2 7.4 fusion.57
  688.9 5.7 reduce.92
  703.4 8.9 convert_bitcast_fusion
  712.3 8.7 copy.218
  720.9 7.5 reshape.1378
  736.4 123.6 %while.33 = (s32[]{:T(128)}, f32[8,516,64]{1,2,0:T(8,128)}, f32[8,1032,64]{1,2,0:T(8,128)}, f32[8,1032,64]{1,2,0:T(8,128)}, pred[1,1032]{1,0:T(4,128)(4,1)S(1)},...) while((s32[]{:T(128)}, f32[8,516,64]{1,2,0:T(8,128)}, ...), condition=%wide.region_27.28_spmd, body=%wide.region_25.27_spmd.sunk | while | flops 345698880 | bytes 17517724 | solution.py:291
  874.2 4.2 reshape.1360
  895.9 5.8 fusion.64
  901.7 4.1 copy.214
  911.2 4.2 convolution_bitcast_fusion.3
  915.4 8.6 copy.184
  925.9 8.4 copy.202
  952.7 34.1 %reduce-scatter.18.cloned.1.call-done = bf16[128,256]{1,0:T(8,128)(2,1)} async-done(((bf16[1024,256]{1,0:T(8,128)(2,1)}), bf16[128,256]{1,0:T(8,128)(2,1)}) %reduce-scatter.18.cloned.1.call-update) | async-done | bytes 65552
  988.4 294.7 %all-reduce.15.cloned.1.call-done = (f32[1,1032,1024]{2,0,1:T(1,128)}, f32[1,1032,1024]{2,0,1:T(1,128)}) async-done(((f32[1,1032,1024]{2,0,1:T(1,128)}, f32[1,1032,1024]{2,0,1:T(1,128)}), (f32[1,1032,1024]{2,0,1:T(1,128)}, f32[1,1032,1024]{2,0,1:T(1,128)})) %all-reduce.15.cloned.1.call-update) | async-done | bytes 8454160
  1294.7 117.4 %all-reduce.13.cloned.1.call-done = (f32[6,1024]{1,0:T(8,128)}, f32[4,1024]{1,0:T(4,128)}, f32[4,2736]{1,0:T(4,128)}) async-done(((f32[6,1024]{1,0:T(8,128)}, f32[4,1024]{1,0:T(4,128)}, f32[4,2736]{1,0:T(4,128)}), (f32[6,1024]{1,0:T(8,128)}, f32[4,1024]{1,0:T(4,128)}, f32[4,2736]{1,0:T(4,128)})) %all-reduce.13.cloned.1.call-update) | async-done | bytes 84752 | tf_op jit(solution)/shard_map/psum | solution.py:355
  (435 shorter events, 321.7 us)
Async XLA Ops:
  7.2 32.2 %all-gather.10.cloned.1.call-start = ((), (), s32[]{:S(2)}) async-start(), calls=%async_computation.8 | async-start | bytes 1769472 | tf_op jit(solution)/shard_map/all_gather | solution.py:123
  7.9 115.0 %all-gather.8.cloned.1.call-start = ((), (), s32[]{:S(2)}) async-start(), calls=%async_computation.7 | async-start | bytes 5283840 | tf_op jit(solution)/shard_map/all_gather | solution.py:14
  14.6 13.2 copy-start.24
  14.6 14.6 %copy-start.40 = (f32[4,1024]{1,0:T(4,128)S(1)}, f32[4,1024]{1,0:T(4,128)}, u32[]{:S(2)}) copy-start(f32[4,1024]{1,0:T(4,128)} %param.23) | copy-start | bytes 49156
  14.6 15.6 %copy-start.38 = (s32[1,2,1032]{2,1,0:T(2,128)S(1)}, s32[1,2,1032]{2,1,0:T(2,128)}, u32[]{:S(2)}) copy-start(s32[1,2,1032]{2,1,0:T(2,128)} %param.27) | copy-start | bytes 24772
  14.6 15.8 %copy-start.39 = (s32[1,1032]{1,0:T(1,128)S(1)}, s32[1,1032]{1,0:T(1,128)}, u32[]{:S(2)}) copy-start(s32[1,1032]{1,0:T(1,128)} %param.25) | copy-start | bytes 12388
  14.6 260.7 %all-gather.12.cloned.1.call-start = ((), (), s32[]{:S(2)}) async-start(), calls=%async_computation.9 | async-start | bytes 2621440 | tf_op jit(solution)/shard_map/all_gather | solution.py:188
  27.8 256.5 %all-gather.16.cloned.1.call-start = ((), (), s32[]{:S(2)}) async-start(), calls=%async_computation.11 | async-start | bytes 3170304 | tf_op jit(solution)/shard_map/all_gather | solution.py:125
  30.3 97.3 %copy-start.26 = (f32[1032]{0:T(1024)}, f32[1032]{0:T(1024)S(1)}, u32[]{:S(2)}) copy-start(f32[1032]{0:T(1024)S(1)} %get-tuple-element.412) | copy-start | bytes 12388
  30.3 97.3 %copy-start.28 = (f32[1032]{0:T(1024)}, f32[1032]{0:T(1024)S(1)}, u32[]{:S(2)}) copy-start(f32[1032]{0:T(1024)S(1)} %get-tuple-element.411) | copy-start | bytes 12388
  30.5 97.1 %copy-start.41 = (f32[32]{0:T(128)}, f32[32]{0:T(128)S(1)}, u32[]{:S(2)}) copy-start(f32[32]{0:T(128)S(1)} %mul.775) | copy-start | bytes 388
  235.5 29.7 %all-to-all-start = ((f32[1,1032,256]{2,0,1:T(1,128)}), f32[1,1032,256]{2,0,1:T(1,128)S(1)}, u32[]{:S(2)}, u32[]{:S(2)}) async-start(f32[1,1032,256]{2,0,1:T(1,128)} %copy.180), calls=%async_computation | async-start | bytes 2113536 | tf_op jit(solution)/shard_map/all_to_all | solution.py:187
  239.0 122.0 %all-gather.14.cloned.1.call-start = ((), (), s32[]{:S(2)}) async-start(), calls=%async_computation.10 | async-start | bytes 5283840 | tf_op jit(solution)/shard_map/all_gather | solution.py:14
  280.5 106.0 %all-gather.18.cloned.1.call-start = ((), (), s32[]{:S(2)}) async-start(), calls=%async_computation.12 | async-start | bytes 1585152 | tf_op jit(solution)/shard_map/all_gather | solution.py:126
  281.1 188.3 %all-gather.20.cloned.1.call-start = ((), (), s32[]{:S(2)}) async-start(), calls=%async_computation.13 | async-start | bytes 5283840 | tf_op jit(solution)/shard_map/all_gather | solution.py:14
  283.2 380.7 %all-reduce.11.cloned.1.call-start = ((), (), s32[]{:S(2)}) async-start(), calls=%async_computation.19 | async-start | bytes 8454144
  490.0 6.6 copy-start.46
  508.6 400.5 %reduce-scatter.14.cloned.1.call-start = ((), (), s32[]{:S(2)}) async-start(), calls=%async_computation.14 | async-start | bytes 2621440 | tf_op jit(solution)/shard_map/reduce_scatter | solution.py:256
  671.8 265.9 %reduce-scatter.22.cloned.1.call-start = ((), (), s32[]{:S(2)}) async-start(), calls=%async_computation.18 | async-start | bytes 1769472
  696.8 31.7 %all-to-all-start.1 = ((bf16[4,2,33024]{2,1,0:T(2,128)(2,1)}), bf16[4,2,33024]{2,1,0:T(2,128)(2,1)S(1)}, u32[]{:S(2)}, u32[]{:S(2)}) async-start(bf16[4,2,33024]{2,1,0:T(2,128)(2,1)} %reshape.1429), calls=%async_computation.1 | async-start | bytes 1056768 | tf_op jit(solution)/shard_map/all_to_all | solution.py:253
  700.3 239.3 %reduce-scatter.20.cloned.1.call-start = ((), (), s32[]{:S(2)}) async-start(), calls=%async_computation.17 | async-start | bytes 3244032
  728.5 222.1 %reduce-scatter.16.cloned.1.call-start = ((), (), s32[]{:S(2)}) async-start(), calls=%async_computation.15 | async-start | bytes 1769472
  909.0 77.8 %reduce-scatter.18.cloned.1.call-start = ((), (), s32[]{:S(2)}) async-start(), calls=%async_computation.16 | async-start | bytes 589824
  911.1 372.0 %all-reduce.15.cloned.1.call-start = ((), (), s32[]{:S(2)}) async-start(), calls=%async_computation.21 | async-start | bytes 16908288
  915.4 8.7 copy-start.21
  915.4 8.7 copy-start.23
  915.4 8.7 copy-start.47
  934.4 477.7 %all-reduce.13.cloned.1.call-start = ((), (), s32[]{:S(2)}) async-start(), calls=%async_computation.20 | async-start | bytes 188416 | tf_op jit(solution)/shard_map/psum | solution.py:355
  951.8 333.8 %copy-start.4 = (bf16[1,258,1024]{2,1,0:T(8,128)(2,1)S(1)}, bf16[1,258,1024]{2,1,0:T(8,128)(2,1)}, u32[]{:S(2)}) copy-start(bf16[1,258,1024]{2,1,0:T(8,128)(2,1)} %param.16) | copy-start | bytes 1585156
  951.8 333.8 %copy-start.32 = (f32[1,1024]{1,0:T(1,128)S(1)}, f32[1,1024]{1,0:T(1,128)}, u32[]{:S(2)}) copy-start(f32[1,1024]{1,0:T(1,128)} %copy-done.31) | copy-start | bytes 12292
  951.8 333.8 %copy-start.34 = (f32[258]{0:T(512)S(1)}, f32[258]{0:T(512)}, u32[]{:S(2)}) copy-start(f32[258]{0:T(512)} %copy-done.33) | copy-start | bytes 3100
  951.8 333.8 %copy-start.36 = (f32[258]{0:T(512)S(1)}, f32[258]{0:T(512)}, u32[]{:S(2)}) copy-start(f32[258]{0:T(512)} %copy-done.35) | copy-start | bytes 3100
  (34 other events, 76.3 us)
Sparse Core Ops, SparseCore 0:
  9.9 29.4 all-gather.9
  41.5 81.3 all-gather.7
  124.5 44.4 all-gather.11
  171.3 30.1 all-gather.15
  280.6 80.3 all-gather.13
  362.7 23.6 all-gather.17
  388.0 81.2 all-gather.19
  508.7 155.0 all-reduce.10
  671.9 51.1 reduce-scatter.13
  726.6 38.3 reduce-scatter.21
  768.7 44.8 reduce-scatter.19
  909.1 39.8 reduce-scatter.15
  952.7 34.0 reduce-scatter.17
  989.4 293.6 all-reduce.14
  1291.2 120.8 all-reduce.12
where the time goes:
time: 1440 us; the launch traced here: 1420 us
  waiting for transfers between devices  882 us (61%)
  local copies, waits for them, and re-layouts  183 us (13%)
  matrix products  174 us (12%)
  other arithmetic  74.3 us (5%)
  loops' own time  53.1 us (4%)
  blocking collectives  31.6 us (2%)
  between operations  16.5 us (1%)
    unnamed x21, waiting for transfers between devices  483 us
    all_gather x3, waiting for transfers between devices, gather_rows(): return lax.all_gather(rows_in, 'tensor', axis=1, tiled=True)  243 us
    psum x1, waiting for transfers between devices, on_device(): lax.psum((norm_grads, head_grads, ffn_grads), ('dp', 'tensor'))  117 us
    unnamed x126, local copies, waits for them, and re-layouts  58.5 us
    another operation x1, loops' own time, on_device(): d_query_b, d_key_b, d_value_b = lax.map(attend_back, jnp.arange(item_count))  31.6 us
    dot_general x16, matrix products, block_probs(): lax.dot_general(query_blk, key_all, (((1,), (1,)), ((), ())), preferred_e...  29.1 us
  transfers between devices with their start and end apart: 17, of which 10 were waited for; matrix products, arithmetic and copies ran while one was open for 27% of the time, Pallas kernels for 0%

commit v1 on v0

v1 whole, which is shorter than its diff:
```python
import functools
import math

import jax
import jax.numpy as jnp
from jax import lax
from jax.experimental import pallas as pl
from jax.experimental.pallas import tpu as pltpu
from jax.sharding import PartitionSpec as P

FF = 2730
HD = 64
FF_PAD = 2736
LANES = 128
EPS = 1e-06
VMEM_LIMIT = 44 * 2**20
BF = jnp.bfloat16
F32 = jnp.float32
NT = (((1,), (1,)), ((), ()))
TN = (((0,), (0,)), ((), ()))


def ring_up(value, size):
    return lax.ppermute(value, "tensor", [(j, (j + 1) % size) for j in range(size)])


def ring_down(value, size):
    return lax.ppermute(value, "tensor", [(j, (j - 1) % size) for j in range(size)])


def ring_offsets(size):
    ups = size // 2
    return [0] + [-s for s in range(1, ups + 1)] + [s for s in range(1, size - ups)]


def ring_gather(own, size):
    ups = size // 2
    downs = size - 1 - ups
    upper, lower = [], []
    up_now, down_now = own, own
    for s in range(ups):
        up_now = ring_up(up_now, size)
        upper.append(up_now)
        if s < downs:
            down_now = ring_down(down_now, size)
            lower.append(down_now)
    return [own] + upper + lower


def add_low(left, right):
    return (left.astype(F32) + right.astype(F32)).astype(BF)


def ring_scatter(pieces, size):
    ups = size // 2
    downs = size - 1 - ups
    if size == 1:
        return pieces
    place = {offset % size: at for at, offset in enumerate(ring_offsets(size))}
    up_now = pieces[place[ups % size]]
    down_now = pieces[place[-downs % size]] if downs else None
    for s in range(ups, 0, -1):
        up_now = ring_up(up_now, size)
        if s > 1:
            up_now = add_low(up_now, pieces[place[s - 1]])
        if s <= downs:
            down_now = ring_down(down_now, size)
            if s > 1:
                down_now = add_low(down_now, pieces[place[(1 - s) % size]])
    return [pieces[0], up_now] + ([down_now] if downs else [])


def dp_bits(size):
    bits = []
    step = 2
    while step < size:
        bits.append(step)
        step *= 2
    return bits + ([1] if size > 1 else [])


def flip(value, bit, size):
    return lax.ppermute(value, "dp", [(j, j ^ bit) for j in range(size)])


def dp_gather(block, size):
    stacked = block[None]
    for bit in dp_bits(size):
        stacked = jnp.concatenate([stacked, flip(stacked, bit, size)], axis=0)
    return stacked


def dp_order(size):
    order = [0]
    for bit in dp_bits(size):
        order = order + [at ^ bit for at in order]
    return jnp.array(order, jnp.int32) ^ lax.axis_index("dp")


def dp_scatter(blocks, size):
    if size == 1:
        return blocks[0].astype(F32)
    parity = lax.axis_index("dp") % 2
    pairs = blocks.reshape((size // 2, 2) + blocks.shape[1:])
    away = lax.dynamic_index_in_dim(pairs, 1 - parity, 1, keepdims=False)
    kept = lax.dynamic_index_in_dim(pairs, parity, 1, keepdims=False)
    merged = add_low(kept, flip(away, 1, size))
    groups = [[j for j in range(size) if j % 2 == c] for c in range(2)]
    parts = lax.all_to_all(
        merged, "dp", split_axis=0, concat_axis=0, tiled=True, axis_index_groups=groups
    )
    return jnp.sum(parts.astype(F32), axis=0)


def sum_everywhere(value, dp_size, tensor_size):
    for bit in reversed(dp_bits(dp_size)):
        value = value + flip(value, bit, dp_size)
    step = 1
    while step < tensor_size:
        value = value + lax.ppermute(
            value, "tensor", [(j, j ^ step) for j in range(tensor_size)]
        )
        step *= 2
    return value


def whole(shape):
    return pl.BlockSpec(shape, lambda *_: (0,) * len(shape))


def lead(shape):
    return pl.BlockSpec((1,) + shape, lambda s, *_: (s,) + (0,) * len(shape))


def ordered(shape):
    return pl.BlockSpec((1,) + shape, lambda s, order: (order[s],) + (0,) * len(shape))


def call(body, args, specs, outs, out_specs, grid, scratch=(), prefetch=0, flops=0):
    moved = sum(a.size * a.dtype.itemsize for a in args)
    moved += sum(math.prod(o.shape) * jnp.dtype(o.dtype).itemsize for o in outs)
    return pl.pallas_call(
        body,
        out_shape=outs,
        grid_spec=pltpu.PrefetchScalarGridSpec(
            num_scalar_prefetch=prefetch,
            grid=grid,
            in_specs=specs,
            out_specs=out_specs,
            scratch_shapes=list(scratch),
        ),
        compiler_params=pltpu.CompilerParams(vmem_limit_bytes=VMEM_LIMIT),
        cost_estimate=pl.CostEstimate(
            flops=int(flops), bytes_accessed=int(moved), transcendentals=0
        ),
    )(*args)


def sds(shape, dtype):
    return jax.ShapeDtypeStruct(shape, dtype)


def row_stats(rows, count):
    mean = jnp.sum(rows, axis=1, keepdims=True) / count
    power = jnp.sum(rows * rows, axis=1, keepdims=True) / count
    return mean, lax.rsqrt(power - mean * mean + EPS)


def rows_back(upstream, gain, unit, inv, count):
    scaled = upstream * gain
    first = jnp.sum(scaled, axis=1, keepdims=True) / count
    second = jnp.sum(scaled * unit, axis=1, keepdims=True) / count
    return inv * (scaled - first - unit * second)


def down_sum(rows):
    return jnp.sum(rows, axis=0, keepdims=True)


def put_back_body(order_ref, in_ref, out_ref):
    out_ref[...] = in_ref[0]


def put_back(order, stacked, axis):
    size = stacked.shape[0]
    block = stacked.shape[1:]
    shape = tuple(n * size if at == axis else n for at, n in enumerate(block))
    if block[axis] % (LANES if axis == len(block) - 1 else 16):
        placed = jnp.zeros_like(stacked).at[order].set(stacked)
        return jnp.moveaxis(placed, 0, axis).reshape(shape)
    return call(
        put_back_body,
        (order, stacked),
        [pl.BlockSpec((1,) + block, lambda r, order: (r,) + (0,) * len(block))],
        [sds(shape, stacked.dtype)],
        [
            pl.BlockSpec(
                block,
                lambda r, order: tuple(order[r] if at == axis else 0 for at in range(len(block))),
            )
        ],
        (size,),
        prefetch=1,
    )[0]


def first_norm_body(tokens_ref, dy_ref, keep_ref, norm_ref, normed_ref, low_ref):
    rows = tokens_ref[...].astype(F32)
    mean, inv = row_stats(rows, rows.shape[1])
    normed_ref[...] = ((rows - mean) * inv * norm_ref[0:1, :] + norm_ref[1:2, :]).astype(BF)
    low_ref[...] = (keep_ref[...] * dy_ref[...].astype(F32)).astype(BF)


def spread(table, width):
    return table if width == LANES else jnp.concatenate([table] * (width // LANES), axis=1)


def turn_pairs(rows):
    width = rows.shape[1]
    even = lax.broadcasted_iota(jnp.int32, (1, width), 1) % 2 == 0
    return jnp.where(even, -pltpu.roll(rows, width - 1, 1), pltpu.roll(rows, 1, 1))


def project_body(count, *refs):
    chunk_refs = refs[:count]
    w_ref, head_ref, cos_ref, sin_ref, q_ref, k_ref, v_ref, held = refs[count:]
    for at in range(count):

        @pl.when(pl.program_id(0) == at)
        def _():
            held[...] = chunk_refs[at][...]

    rows = held[...]
    width = w_ref.shape[2]
    cosine, sine = spread(cos_ref[0], width), spread(sin_ref[0], width)
    query = jnp.dot(rows, w_ref[0], preferred_element_type=F32) + head_ref[0:1, :]
    key = jnp.dot(rows, w_ref[1], preferred_element_type=F32)
    value = jnp.dot(rows, w_ref[2], preferred_element_type=F32) + head_ref[1:2, :]
    query_low = (query * cosine + turn_pairs(query) * sine).astype(BF)
    q_ref[0] = (query_low.astype(F32) * HD ** (-0.5)).astype(BF)
    k_ref[0] = (key * cosine + turn_pairs(key) * sine).astype(BF)
    v_ref[0] = value.astype(BF)


def head_lanes(width, head):
    lane = lax.broadcasted_iota(jnp.int32, (1, width), 1)
    return (lane >= head * HD) & (lane < (head + 1) * HD)


def attend_body(order_ref, q_ref, k_ref, v_ref, bias_ref, mixed_ref, lse_ref):
    query, keys, values, bias = q_ref[...], k_ref[...], v_ref[...], bias_ref[...]
    length, width = query.shape
    total = jnp.zeros((length, width), F32)
    for head in range(width // HD):
        mine = head_lanes(width, head)
        query_h = jnp.where(mine, query, jnp.zeros_like(query))
        scores = lax.dot_general(query_h, keys, NT, preferred_element_type=F32) + bias
        row_max = jnp.max(scores, axis=1, keepdims=True)
        exp_score = jnp.exp(scores - row_max)
        row_total = jnp.sum(exp_score, axis=1, keepdims=True)
        out = jnp.dot(exp_score.astype(BF), values, preferred_element_type=F32)
        total = jnp.where(mine, out * (1.0 / row_total), total)
        lse_ref[0, head : head + 1, :] = (row_max + jnp.log(row_total)).reshape(1, length)
    rows = mixed_ref.shape[1]
    for part in range(length // rows):
        at = order_ref[pl.program_id(0) * (length // rows) + part]
        mixed_ref[at] = total[part * rows : (part + 1) * rows].astype(BF)


def attend_back_body(
    order_ref,
    q_ref,
    dmix_ref,
    lse_ref,
    k_ref,
    v_ref,
    bias_ref,
    cos_ref,
    sin_ref,
    coss_ref,
    sins_ref,
    dq_ref,
    dk_ref,
    dv_ref,
    sums_ref,
    dk_sum,
    dv_sum,
):
    step = pl.program_id(0)

    @pl.when(step == 0)
    def _():
        dk_sum[...] = jnp.zeros_like(dk_sum)
        dv_sum[...] = jnp.zeros_like(dv_sum)
        sums_ref[...] = jnp.zeros_like(sums_ref)

    query, keys, values, bias = q_ref[...], k_ref[...], v_ref[...], bias_ref[...]
    length, width = query.shape
    rows = dmix_ref.shape[1]
    parts = length // rows
    d_mixed = jnp.concatenate([dmix_ref[order_ref[step * parts + p]] for p in range(parts)], axis=0)
    total = jnp.zeros((length, width), F32)
    for head in range(width // HD):
        mine = head_lanes(width, head)
        zero = jnp.zeros_like(query)
        query_h, d_mixed_h = jnp.where(mine, query, zero), jnp.where(mine, d_mixed, zero)
        scores = lax.dot_general(keys, query_h, NT, preferred_element_type=F32) + bias
        probs = jnp.exp(scores - lse_ref[0, head : head + 1, :])
        d_probs = lax.dot_general(values, d_mixed_h, NT, preferred_element_type=F32)
        d_scores = (probs * (d_probs - down_sum(probs * d_probs))).astype(BF)
        dv_sum[...] += jnp.dot(probs.astype(BF), d_mixed_h, preferred_element_type=F32)
        dk_sum[...] += jnp.dot(d_scores, query_h, preferred_element_type=F32)
        d_query = lax.dot_general(d_scores, keys, TN, preferred_element_type=F32)
        total = jnp.where(mine, d_query, total)
    total = total * HD ** (-0.5)
    cosine, sine = spread(cos_ref[...], width), spread(sin_ref[...], width)
    d_query_pre = (total * cosine - turn_pairs(total) * sine).astype(BF)
    dq_ref[...] = d_query_pre
    sums_ref[0:1, :] += down_sum(d_query_pre.astype(F32))

    @pl.when(step == pl.num_programs(0) - 1)
    def _():
        d_key = dk_sum[...]
        all_cos, all_sin = spread(coss_ref[...], width), spread(sins_ref[...], width)
        dk_ref[...] = (d_key * all_cos - turn_pairs(d_key) * all_sin).astype(BF)
        d_value_pre = dv_sum[...].astype(BF)
        dv_ref[...] = d_value_pre
        sums_ref[1:2, :] = down_sum(d_value_pre.astype(F32))


def mixed_rows(mixed_ref):
    parts = mixed_ref.shape[0]
    return jnp.concatenate([mixed_ref[p] for p in range(parts)], axis=1).astype(F32)


def middle_body(
    mixed_ref, tokens_ref, keep_ref, w_ref, norm_ref, head_ref, inner_ref, middle_ref, normed_ref
):
    mixed = mixed_rows(mixed_ref)
    mean, inv = row_stats(mixed, mixed.shape[1])
    inner = ((mixed - mean) * inv * head_ref[2:3, :] + head_ref[3:4, :]).astype(BF)
    inner_ref[...] = inner
    branch = jnp.dot(inner, w_ref[...], preferred_element_type=F32) + norm_ref[4:5, :]
    middle = tokens_ref[...].astype(F32) + keep_ref[...] * branch
    middle_ref[...] = middle
    mean, inv = row_stats(middle, middle.shape[1])
    normed_ref[...] = ((middle - mean) * inv * norm_ref[2:3, :] + norm_ref[3:4, :]).astype(BF)


def sigmoid(gate):
    return 1.0 / (1.0 + jnp.exp(-gate))


def ffn_body(count, order_ref, *refs):
    x_refs, e_refs = refs[:count], refs[count : 2 * count]
    (w_gu_ref, w_down_ref, ffn_ref, unit_ref, gate_ref, up_ref, d_ref, stats_ref, x_held, e_held) = (
        refs[2 * count :]
    )
    for at in range(count):

        @pl.when(pl.program_id(0) == at)
        def _():
            x_held[...] = x_refs[at][...]
            e_held[...] = e_refs[at][...]

    rows = x_held[...]
    gate = jnp.dot(rows, w_gu_ref[0], preferred_element_type=F32) + ffn_ref[0:1, :]
    up = jnp.dot(rows, w_gu_ref[1], preferred_element_type=F32) + ffn_ref[1:2, :]
    d_ffn = lax.dot_general(e_held[...], w_down_ref[...], NT, preferred_element_type=F32)
    gate_ref[0], up_ref[0], d_ref[0] = gate, up, d_ffn
    unit = unit_ref[...]
    hidden = gate * sigmoid(gate) * up
    masked = hidden * unit
    scaled = d_ffn * ffn_ref[2:3, :] * unit
    length = rows.shape[0]
    for at, term in enumerate((masked, masked * hidden, scaled, scaled * hidden)):
        stats_ref[0, at : at + 1, :] = jnp.sum(term, axis=1, keepdims=True).reshape(1, length)


def ffn_back_body(count, order_ref, *refs):
    gate_ref, up_ref, d_ref, stats_ref, w_gu_ref, ffn_ref, unit_ref = refs[:7]
    low_ref, dgate_ref, dup_ref, sums_ref = refs[7:11]
    out_refs = refs[11:]
    step = pl.program_id(0)

    @pl.when(step == 0)
    def _():
        sums_ref[...] = jnp.zeros_like(sums_ref)

    gate, up, d_ffn, unit = gate_ref[0], up_ref[0], d_ref[0], unit_ref[...]
    gain = ffn_ref[2:3, :]
    stats = stats_ref[0]
    mean = stats[:, 0:1] / FF
    inv = lax.rsqrt(stats[:, 1:2] / FF - mean * mean + EPS)
    first = stats[:, 2:3]
    second = inv * (stats[:, 3:4] - mean * first)
    sig = sigmoid(gate)
    silu = gate * sig
    unit_value = (silu * up - mean) * inv
    low_ref[0] = (unit * (unit_value * gain + ffn_ref[3:4, :])).astype(BF)
    d_hidden = unit * inv * (d_ffn * gain * unit - first / FF - unit_value * (second / FF))
    d_gate = (d_hidden * up * sig * (1.0 + gate * (1.0 - sig))).astype(BF)
    d_up = (d_hidden * silu).astype(BF)
    dgate_ref[0], dup_ref[0] = d_gate, d_up
    d_masked = d_ffn * unit
    sums_ref[0:1, :] += down_sum(d_gate.astype(F32))
    sums_ref[1:2, :] += down_sum(d_up.astype(F32))
    sums_ref[2:3, :] += down_sum(d_masked * unit_value)
    sums_ref[3:4, :] += down_sum(d_masked)
    out = lax.dot_general(d_gate, w_gu_ref[0], NT, preferred_element_type=F32)
    out += lax.dot_general(d_up, w_gu_ref[1], NT, preferred_element_type=F32)
    for at in range(count):

        @pl.when(step == at)
        def _():
            out_refs[at][...] = out.astype(BF)


def down_body(count, low_ref, w_ref, *out_refs):
    out = jnp.dot(low_ref[0], w_ref[...], preferred_element_type=F32)
    for at in range(count):

        @pl.when(pl.program_id(0) == at)
        def _():
            out_refs[at][...] = out.astype(BF)


def spread_back_body(count, dq_ref, dk_ref, dv_ref, w_ref, *out_refs):
    out = lax.dot_general(dq_ref[...], w_ref[0], NT, preferred_element_type=F32)
    out += lax.dot_general(dk_ref[...], w_ref[1], NT, preferred_element_type=F32)
    out += lax.dot_general(dv_ref[...], w_ref[2], NT, preferred_element_type=F32)
    for at in range(count):

        @pl.when(pl.program_id(0) == at)
        def _():
            out_refs[at][...] = out.astype(BF)


def add_terms(term_refs):
    total = term_refs[0][...].astype(F32)
    for ref in term_refs[1:]:
        total += ref[...].astype(F32)
    return total


def middle_back_body(count, *refs):
    upstream = add_terms(refs[:count])
    middle_ref, dy_ref, low_ref, keep_ref, mixed_ref, w_ref, norm_ref, head_ref = refs[
        count : count + 8
    ]
    dmid_ref, dbranch_ref, dmix_ref, sums_ref = refs[count + 8 :]
    middle = middle_ref[...]
    width = middle.shape[1]
    mean, inv = row_stats(middle, width)
    unit = (middle - mean) * inv
    d_middle = dy_ref[...].astype(F32) + rows_back(upstream, norm_ref[2:3, :], unit, inv, width)
    dmid_ref[...] = d_middle
    sums_ref[0:1, :] = down_sum(upstream * unit)
    sums_ref[1:2, :] = down_sum(upstream)
    d_branch = (keep_ref[...] * d_middle).astype(BF)
    dbranch_ref[...] = d_branch
    sums_ref[2:3, :] = down_sum(d_branch.astype(F32))
    sums_ref[3:4, :] = down_sum(low_ref[...].astype(F32))
    d_inner = lax.dot_general(d_branch, w_ref[...], NT, preferred_element_type=F32)
    mixed = mixed_rows(mixed_ref)
    mean, inv = row_stats(mixed, width)
    unit = (mixed - mean) * inv
    d_mixed = rows_back(d_inner, head_ref[2:3, :], unit, inv, width).astype(BF)
    part = mixed_ref.shape[2]
    for at in range(mixed_ref.shape[0]):
        dmix_ref[at] = d_mixed[:, at * part : (at + 1) * part]
    sums_ref[4:5, :] = down_sum(d_inner * unit)
    sums_ref[5:6, :] = down_sum(d_inner)
    sums_ref[6:8, :] = jnp.zeros((2, width), F32)


def first_back_body(count, *refs):
    upstream = add_terms(refs[:count])
    tokens_ref, dmid_ref, norm_ref, out_ref, sums_ref = refs[count:]
    rows = tokens_ref[...].astype(F32)
    width = rows.shape[1]
    mean, inv = row_stats(rows, width)
    unit = (rows - mean) * inv
    d_tokens = dmid_ref[...] + rows_back(upstream, norm_ref[0:1, :], unit, inv, width)
    out_ref[...] = d_tokens[: out_ref.shape[0]]
    sums_ref[0:1, :] = down_sum(upstream * unit)
    sums_ref[1:2, :] = down_sum(upstream)


def layer_out_body(count, *refs):
    branch = add_terms(refs[:count])
    middle_ref, keep_ref, norm_ref, out_ref = refs[count:]
    out = middle_ref[...] + keep_ref[...] * (branch + norm_ref[5:6, :])
    out_ref[...] = out[: out_ref.shape[0]].astype(BF)


def rope_tables(coords):
    half_dim = HD // 2
    index_j = jnp.arange(half_dim // 2).astype(F32)
    frequency = jnp.repeat(jnp.exp(index_j * (-2.0 * math.log(10000.0) / half_dim)), 2)
    frequency = jnp.tile(frequency, LANES // half_dim)
    second = (jnp.arange(LANES) // half_dim) % 2 == 1
    places = coords.astype(F32) * 0.5
    angles = jnp.where(second, places[1][..., None], places[0][..., None]) * frequency
    return jnp.cos(angles), jnp.sin(angles)


def pad_to(value, axis, size):
    widths = [(0, 0)] * value.ndim
    widths[axis] = (0, size - value.shape[axis])
    return jnp.pad(value, widths)


def ceil_to(value, unit):
    return -(-value // unit) * unit


def on_device(
    n_dp,
    n_tp,
    tokens,
    cotangent,
    w_qkv,
    w_o,
    w_gu,
    w_down,
    norm_params,
    head_params,
    ffn_params,
    token_mask,
    empty_flag,
    coords,
):
    tp_index = lax.axis_index("tensor")
    own_rows, width = tokens.shape[1:]
    local = w_qkv.shape[2]
    units = w_gu.shape[2]
    heads = local // HD
    rows = ceil_to(own_rows, 16)
    seq = rows * n_tp
    lanes = ceil_to(units, LANES)
    step_rows = 2 * rows if n_tp % 2 == 0 else rows
    steps = seq // step_rows
    offsets = ring_offsets(n_tp)
    order = (jnp.array(offsets, jnp.int32) + tp_index) % n_tp

    slots = jnp.concatenate([token_mask, coords[0]], axis=0).reshape(3, n_tp, own_rows)
    slots = pad_to(slots, 2, rows)
    slots = jnp.stack(
        [lax.dynamic_index_in_dim(slots, order[at], 1, keepdims=False) for at in range(n_tp)], 1
    )
    mask = slots[0]
    bias = jnp.where(mask > 0, 0.0, -1e30).astype(F32)
    bias_row, bias_col = bias.reshape(1, seq), bias.reshape(seq, 1)
    keep = (mask[0].astype(F32) * (1.0 - empty_flag[0].astype(F32)))[:, None]
    cosine, sine = rope_tables(slots[1:])
    cos_all, sin_all = cosine.reshape(seq, LANES), sine.reshape(seq, LANES)

    head_local = lax.dynamic_slice_in_dim(head_params, tp_index * local, local, 1)
    ffn_local = pad_to(
        lax.dynamic_slice_in_dim(ffn_params, tp_index * units, units, 1), 1, lanes
    )
    lane_at = jnp.arange(lanes)
    unit_row = ((lane_at < units) & (tp_index * units + lane_at < FF)).astype(F32)[None]

    tokens_own = pad_to(tokens[0], 0, rows)
    dy_own = pad_to(cotangent[0], 0, rows)

    normed, d_low = call(
        first_norm_body,
        (tokens_own, dy_own, keep, norm_params),
        [whole((rows, width))] * 2 + [whole((rows, 1)), whole(norm_params.shape)],
        [sds((rows, width), BF)] * 2,
        [whole((rows, width))] * 2,
        (1,),
    )
    normed_parts = ring_gather(normed, n_tp)

    w_order = dp_order(n_dp)
    full_qkv = put_back(w_order, dp_gather(w_qkv, n_dp), 1)
    o_parts = lax.all_gather(w_o, "tensor", axis=0, tiled=True)
    full_o = put_back(w_order, dp_gather(o_parts, n_dp), 1)
    full_gu = put_back(w_order, dp_gather(pad_to(w_gu, 2, lanes), n_dp), 1)
    full_down = put_back(w_order, dp_gather(pad_to(w_down, 0, lanes), n_dp), 1)

    query, key, value = call(
        functools.partial(project_body, n_tp),
        (*normed_parts, full_qkv, head_local, cosine, sine),
        [whole((rows, width))] * n_tp
        + [whole(full_qkv.shape), whole(head_local.shape)]
        + [lead((rows, LANES))] * 2,
        [sds((n_tp, rows, local), BF)] * 3,
        [lead((rows, local))] * 3,
        (n_tp,),
        scratch=[pltpu.VMEM((rows, width), BF)],
        flops=2 * seq * width * 3 * local,
    )
    query, key, value = (part.reshape(seq, local) for part in (query, key, value))
    strip = pl.BlockSpec((step_rows, local), lambda s, *_: (s, 0))
    mixed_heads, lse = call(
        attend_body,
        (order, query, key, value, bias_row),
        [strip, whole((seq, local)), whole((seq, local)), whole((1, seq))],
        [sds((n_tp, rows, local), BF), sds((steps, heads, step_rows), F32)],
        [whole((n_tp, rows, local)), lead((heads, step_rows))],
        (steps,),
        prefetch=1,
        flops=4 * seq * seq * local * 4,
    )
    mixed = lax.all_to_all(mixed_heads, "tensor", split_axis=0, concat_axis=0, tiled=True)
    d_low_parts = ring_gather(d_low, n_tp)

    own = whole((rows, width))
    inner_low, middle, normed_two = call(
        middle_body,
        (mixed, tokens_own, keep, full_o, norm_params, head_params),
        [
            whole(mixed.shape),
            own,
            whole((rows, 1)),
            whole(full_o.shape),
            whole(norm_params.shape),
            whole(head_params.shape),
        ],
        [sds((rows, width), BF), sds((rows, width), F32), sds((rows, width), BF)],
        [own] * 3,
        (1,),
        flops=2 * rows * width * width,
    )
    two_parts = ring_gather(normed_two, n_tp)

    hidden_block = lead((rows, lanes))
    gate, up, d_ffn, stats = call(
        functools.partial(ffn_body, n_tp),
        (order, *two_parts, *d_low_parts, full_gu, full_down, ffn_local, unit_row),
        [own] * (2 * n_tp)
        + [
            whole(full_gu.shape),
            whole(full_down.shape),
            whole(ffn_local.shape),
            whole(unit_row.shape),
        ],
        [sds((n_tp, rows, lanes), F32)] * 3 + [sds((n_tp, 4, rows), F32)],
        [hidden_block] * 3 + [ordered((4, rows))],
        (n_tp,),
        scratch=[pltpu.VMEM((rows, width), BF)] * 2,
        prefetch=1,
        flops=6 * seq * width * lanes,
    )
    stats = jnp.swapaxes(lax.psum(stats, "tensor"), 1, 2)
    outs = call(
        functools.partial(ffn_back_body, n_tp),
        (order, gate, up, d_ffn, stats, full_gu, ffn_local, unit_row),
        [hidden_block] * 3
        + [
            ordered((rows, 4)),
            whole(full_gu.shape),
            whole(ffn_local.shape),
            whole(unit_row.shape),
        ],
        [sds((n_tp, rows, lanes), BF)] * 3
        + [sds((4, lanes), F32)]
        + [sds((rows, width), BF)] * n_tp,
        [hidden_block] * 3 + [whole((4, lanes))] + [own] * n_tp,
        (n_tp,),
        prefetch=1,
        flops=4 * seq * width * lanes,
    )
    ffn_low, d_gate, d_up, ffn_sums = outs[:4]
    d_two_terms = ring_scatter(outs[4:], n_tp)
    branch_parts = call(
        functools.partial(down_body, n_tp),
        (ffn_low, full_down),
        [hidden_block, whole(full_down.shape)],
        [sds((rows, width), BF)] * n_tp,
        [own] * n_tp,
        (n_tp,),
        flops=2 * seq * width * lanes,
    )

    n_terms = len(d_two_terms)
    d_middle, d_branch, d_mixed_rows, mid_sums = call(
        functools.partial(middle_back_body, n_terms),
        (*d_two_terms, middle, dy_own, d_low, keep, mixed, full_o, norm_params, head_params),
        [own] * n_terms
        + [own] * 3
        + [
            whole((rows, 1)),
            whole(mixed.shape),
            whole(full_o.shape),
            whole(norm_params.shape),
            whole(head_params.shape),
        ],
        [
            sds((rows, width), F32),
            sds((rows, width), BF),
            sds((n_tp, rows, local), BF),
            sds((8, width), F32),
        ],
        [own, own, whole((n_tp, rows, local)), whole((8, width))],
        (1,),
        flops=2 * rows * width * width,
    )
    d_mixed = lax.all_to_all(d_mixed_rows, "tensor", split_axis=0, concat_axis=0, tiled=True)
    branch_terms = ring_scatter(branch_parts, n_tp)
    layer_out = call(
        functools.partial(layer_out_body, n_terms),
        (*branch_terms, middle, keep, norm_params),
        [own] * n_terms + [own, whole((rows, 1)), whole(norm_params.shape)],
        [sds((own_rows, width), BF)],
        [whole((own_rows, width))],
        (1,),
    )[0]

    table = pl.BlockSpec((step_rows, LANES), lambda s, *_: (s, 0))
    all_rows = whole((seq, local))
    d_query, d_key, d_value, head_sums = call(
        attend_back_body,
        (
            order,
            query,
            d_mixed,
            lse,
            key,
            value,
            bias_col,
            cos_all,
            sin_all,
            cos_all,
            sin_all,
        ),
        [
            strip,
            whole(d_mixed.shape),
            lead((heads, step_rows)),
            all_rows,
            all_rows,
            whole((seq, 1)),
            table,
            table,
            whole((seq, LANES)),
            whole((seq, LANES)),
        ],
        [sds((seq, local), BF)] * 3 + [sds((8, local), F32)],
        [strip, all_rows, all_rows, whole((8, local))],
        (steps,),
        scratch=[pltpu.VMEM((seq, local), F32)] * 2,
        prefetch=1,
        flops=10 * seq * seq * local * 4,
    )
    chunk = pl.BlockSpec((rows, local), lambda s, *_: (s, 0))
    d_one_parts = call(
        functools.partial(spread_back_body, n_tp),
        (d_query, d_key, d_value, full_qkv),
        [chunk] * 3 + [whole(full_qkv.shape)],
        [sds((rows, width), BF)] * n_tp,
        [own] * n_tp,
        (n_tp,),
        flops=2 * seq * width * 3 * local,
    )
    d_one_terms = ring_scatter(d_one_parts, n_tp)
    d_tokens, one_sums = call(
        functools.partial(first_back_body, n_terms),
        (*d_one_terms, tokens_own, d_middle, norm_params),
        [own] * n_terms + [own, own, whole(norm_params.shape)],
        [sds((own_rows, width), F32), sds((2, width), F32)],
        [whole((own_rows, width)), whole((2, width))],
        (1,),
    )

    def product(left, right):
        out = lax.dot_general(left, right, TN, preferred_element_type=F32).astype(BF)
        return out.reshape(n_dp, width // n_dp, out.shape[1])

    two_all = jnp.concatenate(two_parts, axis=0)
    low_all = jnp.concatenate(d_low_parts, axis=0)
    hidden_rows = [part.reshape(seq, lanes) for part in (d_gate, d_up, ffn_low)]
    grad_ffn = jnp.concatenate(
        [
            product(two_all, hidden_rows[0]),
            product(two_all, hidden_rows[1]),
            product(low_all, hidden_rows[2]),
        ],
        axis=2,
    )
    grad_ffn = dp_scatter(grad_ffn, n_dp)
    grad_gu = jnp.stack([grad_ffn[:, :units], grad_ffn[:, lanes : lanes + units]])
    grad_down = grad_ffn[:, 2 * lanes : 2 * lanes + units].T
    grad_o = dp_scatter(product(d_branch, inner_low), n_dp).astype(BF)
    grad_o = lax.all_to_all(
        grad_o.reshape(grad_o.shape[0], n_tp, local).swapaxes(0, 1),
        "tensor",
        split_axis=0,
        concat_axis=0,
        tiled=True,
    )
    grad_o = jnp.sum(grad_o.astype(F32), axis=0).T
    normed_all = jnp.concatenate(normed_parts, axis=0)
    d_proj = jnp.concatenate([d_query, d_key, d_value], axis=1)
    grad_qkv = dp_scatter(product(normed_all, d_proj), n_dp)
    grad_qkv = grad_qkv.reshape(-1, 3, local).swapaxes(0, 1)

    ffn_canvas = lax.dynamic_update_slice(
        jnp.zeros((4, FF_PAD), F32), ffn_sums[:, :units], (0, tp_index * units)
    )
    early = jnp.concatenate([mid_sums[:6].reshape(-1), ffn_canvas.reshape(-1)])
    early_len = early.shape[0]
    early = pad_to(early, 0, ceil_to(early_len, 8 * LANES)).reshape(-1, LANES)
    early = sum_everywhere(early, n_dp, n_tp).reshape(-1)
    mid_total = early[: 6 * width].reshape(6, width)
    ffn_total = early[6 * width : early_len].reshape(4, FF_PAD)
    head_canvas = lax.dynamic_update_slice(
        jnp.zeros((2, width), F32), head_sums[:2], (0, tp_index * local)
    )
    late = sum_everywhere(jnp.concatenate([one_sums, head_canvas], axis=0), n_dp, n_tp)
    norm_total = jnp.concatenate([late[:2], mid_total[:4]], axis=0)
    head_total = jnp.concatenate([late[2:], mid_total[4:]], axis=0)
    return (
        layer_out[None],
        d_tokens[None],
        grad_qkv,
        grad_o,
        grad_gu,
        grad_down,
        norm_total,
        head_total,
        ffn_total,
    )


def solution(mesh):
    placed = (
        P("dp", "tensor", None),
        P("dp", "tensor", None),
        P(None, "dp", "tensor"),
        P("tensor", "dp"),
        P(None, "dp", "tensor"),
        P("tensor", "dp"),
        P(),
        P(),
        P(),
        P("dp", None),
        P("dp"),
        P("dp", None, None),
    )
    return jax.shard_map(
        functools.partial(on_device, mesh.shape["dp"], mesh.shape["tensor"]),
        mesh=mesh,
        in_specs=placed,
        out_specs=(
            P("dp", "tensor", None),
            P("dp", "tensor", None),
            P(None, "dp", "tensor"),
            P("tensor", "dp"),
            P(None, "dp", "tensor"),
            P("tensor", "dp"),
            P(),
            P(),
            P(),
        ),
        check_vma=False,
    )
```

time: 1440 us -> 508 us (0.35)
  waiting for transfers between devices: 882 us -> 144 us
  matrix products: 174 us -> 13.7 us
  local copies, waits for them, and re-layouts: 183 us -> 43.8 us
  Pallas kernels: 0 us -> 84.7 us
  starting transfers between devices: 8.19 us -> 91.7 us
  loops' own time: 53.1 us -> 0 us
  blocking collectives: 31.6 us -> 59.1 us
  other arithmetic: 74.3 us -> 52.4 us
    unnamed x21 -> x0, waiting for transfers between devices: 483 us -> none
    all_gather x7 -> x0, waiting for transfers between devices: 257 us -> none  [the longest x3 243 us: gather_rows(): return lax.all_gather(rows_in, 'tensor', axis=1, tiled=True)]
    dot_general x68 -> x5, matrix products: 174 us -> 13.7 us  [product(): lax.dot_general(left, right, TN, preferred_element_type=F32).astype(BF)]
    psum x1 -> x0, waiting for transfers between devices: 117 us -> none  [on_device(): lax.psum((norm_grads, head_grads, ffn_grads), ('dp', 'tensor'))]
    ppermute x0 -> x43, waiting for transfers between devices: none -> 107 us  [the longest x12 56.3 us: ring_up(): lax.ppermute(value, 'tensor', [(j, (j + 1) % size) for j in range(size)])]
    pallas_call x0 -> x16, Pallas kernels: none -> 84.7 us  [call(): pl.pallas_call(body, out_shape=outs, grid_spec=pltpu.PrefetchScalarGridSp...]
    ppermute x0 -> x43, starting transfers between devices: none -> 67.8 us  [the longest x12 26.2 us: ring_up(): lax.ppermute(value, 'tensor', [(j, (j + 1) % size) for j in range(size)])]
    another operation x2 -> x0, loops' own time: 53.1 us -> none  [the longest x1 31.6 us: on_device(): d_query_b, d_key_b, d_value_b = lax.map(attend_back, jnp.arange(item_count))]
  transfers between devices with their start and end apart: 17 -> 49, of which waited for: 10 -> 20; matrix products, arithmetic and copies ran while one was open for 27% -> 17% of each run, Pallas kernels for 0% -> 11%
where the time goes in v1:
time: 508 us; the launch traced here: 500 us
  waiting for transfers between devices  144 us (28%)
  starting transfers between devices  91.7 us (18%)
  Pallas kernels  84.7 us (17%)
  blocking collectives  59.1 us (12%)
  other arithmetic  52.4 us (10%)
  local copies, waits for them, and re-layouts  43.8 us (9%)
  matrix products  13.7 us (3%)
  between operations  10.6 us (2%)
    pallas_call x16, Pallas kernels, call(): pl.pallas_call(body, out_shape=outs, grid_spec=pltpu.PrefetchScalarGridSp...  84.7 us
    ppermute x12, waiting for transfers between devices, ring_up(): lax.ppermute(value, 'tensor', [(j, (j + 1) % size) for j in range(size)])  56.3 us
    ppermute x21, waiting for transfers between devices, flip(): return lax.ppermute(value, 'dp', [(j, j ^ bit) for j in range(size)])  35.6 us
    all_gather x1, blocking collectives, on_device(): o_parts = lax.all_gather(w_o, 'tensor', axis=0, tiled=True)  32.5 us
    unnamed x173, local copies, waits for them, and re-layouts  26.7 us
    psum x1, blocking collectives, on_device(): stats = jnp.swapaxes(lax.psum(stats, 'tensor'), 1, 2)  26.6 us
    ppermute x12, starting transfers between devices, ring_up(): lax.ppermute(value, 'tensor', [(j, (j + 1) % size) for j in range(size)])  26.2 us
    concatenate x12, other arithmetic, dp_gather(): stacked = jnp.concatenate([stacked, flip(stacked, bit, size)], axis=0)  21.1 us
  transfers between devices with their start and end apart: 49, of which 20 were waited for; matrix products, arithmetic and copies ran while one was open for 17% of the time, Pallas kernels for 11%

profile of v1, /device:TPU:0, one launch (start us, length us, event | category | flops | bytes accessed | tf_op | source)
XLA Modules:
  0.0 500.3 jit_solution(620262267716627591)
XLA Ops:
  17.5 32.5 %all_gather.3 = bf16[1024,128]{1,0:T(8,128)(2,1)} all-gather(bf16[256,128]{1,0:T(8,128)(2,1)S(1)} %copy-done.80), channel_id=1, replica_groups=mesh['dp'=8,'tensor'=4] {'tensor'}, dimensions={0}, use_global_device_ids=true | all-gather | bytes 327680 | tf_op jit(solution)/shard_map/all_gather | solution.py:581
  86.9 4.3 collective-permute-done.1.refs_2_
  91.3 4.4 shard_map.207
  95.7 11.3 %shard_map.208 = (bf16[4,272,256]{2,1,0:T(8,128)(2,1)}, f32[2,4,544]{2,1,0:T(4,128)S(1)}) custom-call(s32[4]{0:T(128)S(1)} %and_select_fusion.2.order_ref, bf16[1088,256]{1,0:T(8,128)(2,1)S(1)} %bitcast.91, bf16[1088,256]{1,0:T(8,128)(2,1)S(1)} %bitcast.93, bf16[1088,256]{1,0:T(8,128)(2,1)S(1)} %bitcast.95, f32[1,1088]{1,0:T(1,128)S(1)} %select_n.108.bias_ref), custom_call_target="tpu_custom_call" | custom-call | flops 4848615424 | bytes 2250000 | tf_op jit(solution)/shard_map/pallas_call | solution.py:142
  128.2 10.6 %all-to-all-done.mixed_ref.refs_7_ = bf16[4,272,256]{2,1,0:T(8,128)(2,1)S(1)} async-done(((bf16[4,272,256]{2,1,0:T(8,128)(2,1)}), bf16[4,272,256]{2,1,0:T(8,128)(2,1)S(1)}, u32[]{:S(2)}, u32[]{:S(2)}) %all-to-all-start) | async-done | bytes 557088 | tf_op jit(solution)/shard_map/all_to_all | solution.py:610
  142.7 12.2 %collective-permute-start.9 = (bf16[272,1024]{1,0:T(8,128)(2,1)}, bf16[272,1024]{1,0:T(8,128)(2,1)}, u32[]{:S(2)}, u32[]{:S(2)}) collective-permute-start(bf16[272,1024]{1,0:T(8,128)(2,1)} %get-tuple-element.54.refs_0_), channel_id=1, source_target_pairs={{0,1},{1,2},{2,3},{3,0},{4,5},{5,6},{6,7},{7,4},{8,9},{9,10},{10,1... | collective-permute-start | bytes 1671176 | tf_op jit(solution)/shard_map/ppermute | solution.py:24
  163.4 9.4 %collective-permute-done.9.refs_1_ = bf16[272,1024]{1,0:T(8,128)(2,1)} collective-permute-done((bf16[272,1024]{1,0:T(8,128)(2,1)}, bf16[272,1024]{1,0:T(8,128)(2,1)}, u32[]{:S(2)}, u32[]{:S(2)}) %collective-permute-start.9) | collective-permute-done | bytes 557088 | tf_op jit(solution)/shard_map/ppermute | solution.py:24
  184.5 11.8 %collective-permute-done.11.refs_3_ = bf16[272,1024]{1,0:T(8,128)(2,1)S(1)} collective-permute-done((bf16[272,1024]{1,0:T(8,128)(2,1)}, bf16[272,1024]{1,0:T(8,128)(2,1)S(1)}, u32[]{:S(2)}, u32[]{:S(2)}) %collective-permute-start.11) | collective-permute-done | bytes 557088 | tf_op jit(solution)/shard_map/ppermute | solution.py:28
  196.3 8.9 %collective-permute-done.10.refs_2_ = bf16[272,1024]{1,0:T(8,128)(2,1)S(1)} collective-permute-done((bf16[272,1024]{1,0:T(8,128)(2,1)}, bf16[272,1024]{1,0:T(8,128)(2,1)S(1)}, u32[]{:S(2)}, u32[]{:S(2)}) %collective-permute-start.10) | collective-permute-done | bytes 557088 | tf_op jit(solution)/shard_map/ppermute | solution.py:24
  205.2 10.8 %shard_map.213 = (f32[4,272,768]{2,1,0:T(8,128)}, f32[4,272,768]{2,1,0:T(8,128)}, f32[4,272,768]{2,1,0:T(8,128)}, f32[4,4,272]{2,1,0:T(4,128)S(1)}) custom-call(s32[4]{0:T(128)S(1)} %and_select_fusion.2.order_ref, bf16[272,1024]{1,0:T(8,128)(2,1)} %get-tuple-element.54.refs_0_, bf16[272,1024]{1,0:T(8,128)(2,1)} %collective-permute-done.9.refs_1_, ...), custom_call_target="tpu_custom_call" | custom-call | flops 5133828096 | bytes 19234832 | tf_op jit(solution)/shard_map/pallas_call | solution.py:142
  217.1 26.6 %psum.7.refs_3_ = f32[4,272,4]{2,1,0:T(8,128)} all-reduce(f32[4,272,4]{2,1,0:T(8,128)} %bitcast.97), channel_id=1, replica_groups=mesh['dp'=8,'tensor'=4] {'tensor'}, use_global_device_ids=true, to_apply=%region_0.1 | all-reduce | flops 4352 | bytes 34816 | tf_op jit(solution)/shard_map/psum | solution.py:650
  244.8 12.3 %shard_map.214 = (bf16[4,272,768]{2,1,0:T(8,128)(2,1)S(1)}, bf16[4,272,768]{2,1,0:T(8,128)(2,1)S(1)}, bf16[4,272,768]{2,1,0:T(8,128)(2,1)S(1)}, f32[4,768]{1,0:T...) custom-call(s32[4]{0:T(128)S(1)} %and_select_fusion.2.order_ref, ...), custom_call_target="tpu_custom_call" | custom-call | flops 3422552064 | bytes 20459536 | tf_op jit(solution)/shard_map/pallas_call | solution.py:142
  257.2 3.8 collective-permute-start.26
  263.5 3.7 fusion.18
  267.3 7.5 %collective-permute-done.24 = bf16[272,1024]{1,0:T(8,128)(2,1)S(1)} collective-permute-done((bf16[272,1024]{1,0:T(8,128)(2,1)S(1)}, bf16[272,1024]{1,0:T(8,128)(2,1)S(1)}, u32[]{:S(2)}, u32[]{:S(2)}) %collective-permute-start.24) | collective-permute-done | bytes 557088 | tf_op jit(solution)/shard_map/ppermute | solution.py:24
  274.9 5.5 %collective-permute-start.25 = (bf16[272,1024]{1,0:T(8,128)(2,1)S(1)}, bf16[272,1024]{1,0:T(8,128)(2,1)S(1)}, u32[]{:S(2)}, u32[]{:S(2)}) collective-permute-start(bf16[272,1024]{1,0:T(8,128)(2,1)S(1)} %add_convert_fusion.1), channel_id=1, source_target_pairs={{0,1},{1,2},{2,3},{3,0},{4,5},{5,6},{6,7},{7,4},{8,9},{9,10},{10,1... | collective-permute-start | bytes 1671176 | tf_op jit(solution)/shard_map/ppermute | solution.py:24
  285.1 6.7 %collective-permute-done.25.refs_1_ = bf16[272,1024]{1,0:T(8,128)(2,1)S(1)} collective-permute-done((bf16[272,1024]{1,0:T(8,128)(2,1)S(1)}, bf16[272,1024]{1,0:T(8,128)(2,1)S(1)}, u32[]{:S(2)}, u32[]{:S(2)}) %collective-permute-start.25) | collective-permute-done | bytes 557088 | tf_op jit(solution)/shard_map/ppermute | solution.py:24
  308.3 3.7 all-to-all-done.1.dmix_ref
  315.2 24.0 %shard_map.218 = (bf16[1088,256]{1,0:T(8,128)(2,1)S(1)}, bf16[1088,256]{1,0:T(8,128)(2,1)S(1)}, bf16[1088,256]{1,0:T(8,128)(2,1)S(1)}, f32[8,256]{1,0:T(8,128)S(1)}) custom-call(s32[4]{0:T(128)S(1)} %and_select_fusion.2.order_ref, bf16[1088,256]{1,0:T(8,128)(2,1)S(1)} %bitcast.92, bf16[4,272,256]{2,1,0:T(8,128)(2,1)S(1)} %all-to-all-done.1.dmix_ref, ...), custom_call_target="tpu_custom_call" | custom-call | flops 12121538560 | bytes 6157584 | tf_op jit(solution)/shard_map/pallas_call | solution.py:142
  339.3 4.0 fusion.21
  348.0 4.8 all-to-all-start.3
  355.9 11.3 %all-to-all-done.3 = bf16[4,128,1024]{2,1,0:T(8,128)(2,1)S(1)} async-done(((bf16[4,128,1024]{2,1,0:T(8,128)(2,1)}), bf16[4,128,1024]{2,1,0:T(8,128)(2,1)S(1)}, u32[]{:S(2)}, u32[]{:S(2)}) %all-to-all-start.3) | async-done | bytes 1048608 | tf_op jit(solution)/shard_map/all_to_all | solution.py:109
  367.1 4.2 all-to-all-start.2
  373.0 3.7 shard_map.215
  376.9 3.7 collective-permute-start.23
  390.1 3.8 collective-permute-start.29
  397.4 4.3 fusion
  401.7 16.6 %collective-permute-done.27 = bf16[272,1024]{1,0:T(8,128)(2,1)} collective-permute-done((bf16[272,1024]{1,0:T(8,128)(2,1)}, bf16[272,1024]{1,0:T(8,128)(2,1)}, u32[]{:S(2)}, u32[]{:S(2)}) %collective-permute-start.27) | collective-permute-done | bytes 557088 | tf_op jit(solution)/shard_map/ppermute | solution.py:24
  420.3 11.7 %all-to-all-done.4 = bf16[4,128,256]{2,1,0:T(8,128)(2,1)S(1)} async-done(((bf16[4,128,256]{2,1,0:T(8,128)(2,1)}), bf16[4,128,256]{2,1,0:T(8,128)(2,1)S(1)}, u32[]{:S(2)}, u32[]{:S(2)}) %all-to-all-start.4) | async-done | bytes 262176 | tf_op jit(solution)/shard_map/all_to_all | solution.py:790
  432.7 4.5 all-to-all-start.5
  444.5 21.8 %collective-permute-done.40 = f32[136,128]{1,0:T(8,128)S(1)} collective-permute-done((f32[136,128]{1,0:T(8,128)S(1)}, f32[136,128]{1,0:T(8,128)S(1)}, u32[]{:S(2)}, u32[]{:S(2)}) %collective-permute-start.40) | collective-permute-done | bytes 69664 | tf_op jit(solution)/shard_map/ppermute | solution.py:83
  477.1 3.7 collective-permute-done.35
  (356 shorter events, 181.7 us)
Async XLA Ops:
  10.8 63.5 %collective-permute-start = (bf16[272,1024]{1,0:T(8,128)(2,1)S(1)}, bf16[272,1024]{1,0:T(8,128)(2,1)S(1)}, u32[]{:S(2)}, u32[]{:S(2)}) collective-permute-start(bf16[272,1024]{1,0:T(8,128)(2,1)S(1)} %get-tuple-element.49.refs_0_), channel_id=1, source_target_pairs={{0,1},{1,2},{2,3},{3,0},{4,5},{5,6},{6,7},{7,4},{8,9},{9,10},{10,1... | collective-permute-start | bytes 1671176 | tf_op jit(solution)/shard_map/ppermute | solution.py:24
  13.8 73.1 %collective-permute-start.2 = (bf16[272,1024]{1,0:T(8,128)(2,1)S(1)}, bf16[272,1024]{1,0:T(8,128)(2,1)S(1)}, u32[]{:S(2)}, u32[]{:S(2)}) collective-permute-start(bf16[272,1024]{1,0:T(8,128)(2,1)S(1)} %get-tuple-element.49.refs_0_), channel_id=1, source_target_pairs={{0,3},{1,0},{2,1},{3,2},{4,7},{5,4},{6,5},{7,6},{8,11},{9,8},{10,9... | collective-permute-start | bytes 1671176 | tf_op jit(solution)/shard_map/ppermute | solution.py:28
  15.8 44.8 %collective-permute-start.3 = (bf16[1,3,128,256]{3,2,1,0:T(8,128)(2,1)S(1)}, bf16[1,3,128,256]{3,2,1,0:T(8,128)(2,1)S(1)}, u32[]{:S(2)}, u32[]{:S(2)}) collective-permute-start(bf16[1,3,128,256]{3,2,1,0:T(8,128)(2,1)S(1)} %bitcast.101), channel_id=1, source_target_pairs={{0,8},{4,12},{8,0},{12,4},{16,24},{20,28},{24,16},{28,20},{1,9},{5... | collective-permute-start | bytes 589832 | tf_op jit(solution)/shard_map/ppermute | solution.py:83
  54.1 22.1 %collective-permute-start.15 = (bf16[1,2,128,768]{3,2,1,0:T(8,128)(2,1)S(1)}, bf16[1,2,128,768]{3,2,1,0:T(8,128)(2,1)}, u32[]{:S(2)}, u32[]{:S(2)}) collective-permute-start(bf16[1,2,128,768]{3,2,1,0:T(8,128)(2,1)S(1)} %pad_bitcast_fusion), channel_id=1, source_target_pairs={{0,8},{4,12},{8,0},{12,4},{16,24},{20,28},{24,16},{28,20},{1,9},{5... | collective-permute-start | bytes 1179656 | tf_op jit(solution)/shard_map/ppermute | solution.py:83
  76.2 34.3 %collective-permute-start.18 = (bf16[1,768,128]{2,1,0:T(8,128)(2,1)}, bf16[1,768,128]{2,1,0:T(8,128)(2,1)}, u32[]{:S(2)}, u32[]{:S(2)}) collective-permute-start(bf16[1,768,128]{2,1,0:T(8,128)(2,1)} %pad_bitcast_fusion.1), channel_id=1, source_target_pairs={{0,8},{4,12},{8,0},{12,4},{16,24},{20,28},{24,16},{28,20},{1,9},{5... | collective-permute-start | bytes 589832 | tf_op jit(solution)/shard_map/ppermute | solution.py:83
  80.8 33.2 %collective-permute-start.16 = (bf16[2,2,128,768]{3,2,1,0:T(8,128)(2,1)}, bf16[2,2,128,768]{3,2,1,0:T(8,128)(2,1)}, u32[]{:S(2)}, u32[]{:S(2)}) collective-permute-start(bf16[2,2,128,768]{3,2,1,0:T(8,128)(2,1)} %pad_maximum_fusion.8), channel_id=1, source_target_pairs={{0,16},{4,20},{8,24},{12,28},{16,0},{20,4},{24,8},{28,12},{1,17},{... | collective-permute-start | bytes 2359304 | tf_op jit(solution)/shard_map/ppermute | solution.py:83
  84.6 40.6 %collective-permute-start.8 = (bf16[4,1024,128]{2,1,0:T(8,128)(2,1)}, bf16[4,1024,128]{2,1,0:T(8,128)(2,1)}, u32[]{:S(2)}, u32[]{:S(2)}) collective-permute-start(bf16[4,1024,128]{2,1,0:T(8,128)(2,1)} %pad_maximum_fusion.6), channel_id=1, source_target_pairs={{0,4},{4,0},{8,12},{12,8},{16,20},{20,16},{24,28},{28,24},{1,5},{5... | collective-permute-start | bytes 3145736 | tf_op jit(solution)/shard_map/ppermute | solution.py:83
  107.0 31.8 %all-to-all-start = ((bf16[4,272,256]{2,1,0:T(8,128)(2,1)}), bf16[4,272,256]{2,1,0:T(8,128)(2,1)S(1)}, u32[]{:S(2)}, u32[]{:S(2)}) async-start(bf16[4,272,256]{2,1,0:T(8,128)(2,1)} %get-tuple-element.53), calls=%async_computation | async-start | bytes 1114112 | tf_op jit(solution)/shard_map/all_to_all | solution.py:610
  116.5 60.5 %collective-permute-start.17 = (bf16[4,2,128,768]{3,2,1,0:T(8,128)(2,1)}, bf16[4,2,128,768]{3,2,1,0:T(8,128)(2,1)}, u32[]{:S(2)}, u32[]{:S(2)}) collective-permute-start(bf16[4,2,128,768]{3,2,1,0:T(8,128)(2,1)} %pad_maximum_fusion.4), channel_id=1, source_target_pairs={{0,4},{4,0},{8,12},{12,8},{16,20},{20,16},{24,28},{28,24},{1,5},{5... | collective-permute-start | bytes 4718600 | tf_op jit(solution)/shard_map/ppermute | solution.py:83
  116.5 43.0 %collective-permute-start.12 = (bf16[272,1024]{1,0:T(8,128)(2,1)}, bf16[272,1024]{1,0:T(8,128)(2,1)}, u32[]{:S(2)}, u32[]{:S(2)}) collective-permute-start(bf16[272,1024]{1,0:T(8,128)(2,1)} %get-tuple-element.55.refs_4_.refs_5_), channel_id=1, source_target_pairs={{0,1},{1,2},{2,3},{3,0},{4,5},{5,6},{6,7},{7,4},{8,9},{9,10},{10,1... | collective-permute-start | bytes 1671176 | tf_op jit(solution)/shard_map/ppermute | solution.py:24
  118.5 63.0 %collective-permute-start.14 = (bf16[272,1024]{1,0:T(8,128)(2,1)}, bf16[272,1024]{1,0:T(8,128)(2,1)}, u32[]{:S(2)}, u32[]{:S(2)}) collective-permute-start(bf16[272,1024]{1,0:T(8,128)(2,1)} %get-tuple-element.55.refs_4_.refs_5_), channel_id=1, source_target_pairs={{0,3},{1,0},{2,1},{3,2},{4,7},{5,4},{6,5},{7,6},{8,11},{9,8},{10,9... | collective-permute-start | bytes 1671176 | tf_op jit(solution)/shard_map/ppermute | solution.py:28
  125.1 34.6 %collective-permute-start.20 = (bf16[4,768,128]{2,1,0:T(8,128)(2,1)}, bf16[4,768,128]{2,1,0:T(8,128)(2,1)}, u32[]{:S(2)}, u32[]{:S(2)}) collective-permute-start(bf16[4,768,128]{2,1,0:T(8,128)(2,1)} %pad_maximum_fusion.9), channel_id=1, source_target_pairs={{0,4},{4,0},{8,12},{12,8},{16,20},{20,16},{24,28},{28,24},{1,5},{5... | collective-permute-start | bytes 2359304 | tf_op jit(solution)/shard_map/ppermute | solution.py:83
  142.7 30.1 %collective-permute-start.9 = (bf16[272,1024]{1,0:T(8,128)(2,1)}, bf16[272,1024]{1,0:T(8,128)(2,1)}, u32[]{:S(2)}, u32[]{:S(2)}) collective-permute-start(bf16[272,1024]{1,0:T(8,128)(2,1)} %get-tuple-element.54.refs_0_), channel_id=1, source_target_pairs={{0,1},{1,2},{2,3},{3,0},{4,5},{5,6},{6,7},{7,4},{8,9},{9,10},{10,1... | collective-permute-start | bytes 1671176 | tf_op jit(solution)/shard_map/ppermute | solution.py:24
  159.5 25.0 %collective-permute-start.13 = (bf16[272,1024]{1,0:T(8,128)(2,1)}, bf16[272,1024]{1,0:T(8,128)(2,1)S(1)}, u32[]{:S(2)}, u32[]{:S(2)}) collective-permute-start(bf16[272,1024]{1,0:T(8,128)(2,1)} %collective-permute-done.12.refs_5_), channel_id=1, source_target_pairs={{0,1},{1,2},{2,3},{3,0},{4,5},{5,6},{6,7},{7,4},{8,9},{9,10},{10,1... | collective-permute-start | bytes 1671176 | tf_op jit(solution)/shard_map/ppermute | solution.py:24
  159.7 36.6 %collective-permute-start.11 = (bf16[272,1024]{1,0:T(8,128)(2,1)}, bf16[272,1024]{1,0:T(8,128)(2,1)S(1)}, u32[]{:S(2)}, u32[]{:S(2)}) collective-permute-start(bf16[272,1024]{1,0:T(8,128)(2,1)} %get-tuple-element.54.refs_0_), channel_id=1, source_target_pairs={{0,3},{1,0},{2,1},{3,2},{4,7},{5,4},{6,5},{7,6},{8,11},{9,8},{10,9... | collective-permute-start | bytes 1671176 | tf_op jit(solution)/shard_map/ppermute | solution.py:28
  172.8 32.4 %collective-permute-start.10 = (bf16[272,1024]{1,0:T(8,128)(2,1)}, bf16[272,1024]{1,0:T(8,128)(2,1)S(1)}, u32[]{:S(2)}, u32[]{:S(2)}) collective-permute-start(bf16[272,1024]{1,0:T(8,128)(2,1)} %collective-permute-done.9.refs_1_), channel_id=1, source_target_pairs={{0,1},{1,2},{2,3},{3,0},{4,5},{5,6},{6,7},{7,4},{8,9},{9,10},{10,1... | collective-permute-start | bytes 1671176 | tf_op jit(solution)/shard_map/ppermute | solution.py:24
  257.1 17.6 %collective-permute-start.24 = (bf16[272,1024]{1,0:T(8,128)(2,1)S(1)}, bf16[272,1024]{1,0:T(8,128)(2,1)S(1)}, u32[]{:S(2)}, u32[]{:S(2)}) collective-permute-start(bf16[272,1024]{1,0:T(8,128)(2,1)S(1)} %get-tuple-element.67), channel_id=1, source_target_pairs={{0,1},{1,2},{2,3},{3,0},{4,5},{5,6},{6,7},{7,4},{8,9},{9,10},{10,1... | collective-permute-start | bytes 1671176 | tf_op jit(solution)/shard_map/ppermute | solution.py:24
  257.2 27.9 %collective-permute-start.26 = (bf16[272,1024]{1,0:T(8,128)(2,1)S(1)}, bf16[272,1024]{1,0:T(8,128)(2,1)S(1)}, u32[]{:S(2)}, u32[]{:S(2)}) collective-permute-start(bf16[272,1024]{1,0:T(8,128)(2,1)S(1)} %get-tuple-element.69), channel_id=1, source_target_pairs={{0,3},{1,0},{2,1},{3,2},{4,7},{5,4},{6,5},{7,6},{8,11},{9,8},{10,9... | collective-permute-start | bytes 1671176 | tf_op jit(solution)/shard_map/ppermute | solution.py:28
  304.7 85.4 %collective-permute-start.32 = (bf16[4,128,2304]{2,1,0:T(8,128)(2,1)}, bf16[4,128,2304]{2,1,0:T(8,128)(2,1)}, u32[]{:S(2)}, u32[]{:S(2)}) collective-permute-start(bf16[4,128,2304]{2,1,0:T(8,128)(2,1)} %dynamic-slice_bitcast_fusion), channel_id=1, source_target_pairs={{0,4},{4,0},{8,12},{12,8},{16,20},{20,16},{24,28},{28,24},{1,5},{5... | collective-permute-start | bytes 7077896 | tf_op jit(solution)/shard_map/ppermute | solution.py:83
  307.8 37.6 %collective-permute-start.31 = (bf16[4,128,1024]{2,1,0:T(8,128)(2,1)}, bf16[4,128,1024]{2,1,0:T(8,128)(2,1)}, u32[]{:S(2)}, u32[]{:S(2)}) collective-permute-start(bf16[4,128,1024]{2,1,0:T(8,128)(2,1)} %dynamic-slice_bitcast_fusion.1), channel_id=1, source_target_pairs={{0,4},{4,0},{8,12},{12,8},{16,20},{20,16},{24,28},{28,24},{1,5},{5... | collective-permute-start | bytes 3145736 | tf_op jit(solution)/shard_map/ppermute | solution.py:83
  348.0 19.1 %all-to-all-start.3 = ((bf16[4,128,1024]{2,1,0:T(8,128)(2,1)}), bf16[4,128,1024]{2,1,0:T(8,128)(2,1)S(1)}, u32[]{:S(2)}, u32[]{:S(2)}) async-start(bf16[4,128,1024]{2,1,0:T(8,128)(2,1)} %fusion.17), calls=%async_computation.3 | async-start | bytes 2097152 | tf_op jit(solution)/shard_map/all_to_all | solution.py:109
  367.1 26.8 %all-to-all-start.2 = ((bf16[4,128,768]{2,1,0:T(8,128)(2,1)}), bf16[4,128,768]{2,1,0:T(8,128)(2,1)}, u32[]{:S(2)}, u32[]{:S(2)}) async-start(bf16[4,128,768]{2,1,0:T(8,128)(2,1)} %fusion.29), calls=%async_computation.2 | async-start | bytes 1572864 | tf_op jit(solution)/shard_map/all_to_all | solution.py:109
  376.7 63.5 %collective-permute-start.21 = (bf16[272,1024]{1,0:T(8,128)(2,1)}, bf16[272,1024]{1,0:T(8,128)(2,1)}, u32[]{:S(2)}, u32[]{:S(2)}) collective-permute-start(bf16[272,1024]{1,0:T(8,128)(2,1)} %get-tuple-element.62), channel_id=1, source_target_pairs={{0,1},{1,2},{2,3},{3,0},{4,5},{5,6},{6,7},{7,4},{8,9},{9,10},{10,1... | collective-permute-start | bytes 1671176 | tf_op jit(solution)/shard_map/ppermute | solution.py:24
  376.9 109.5 %collective-permute-start.23 = (bf16[272,1024]{1,0:T(8,128)(2,1)}, bf16[272,1024]{1,0:T(8,128)(2,1)}, u32[]{:S(2)}, u32[]{:S(2)}) collective-permute-start(bf16[272,1024]{1,0:T(8,128)(2,1)} %get-tuple-element.64), channel_id=1, source_target_pairs={{0,3},{1,0},{2,1},{3,2},{4,7},{5,4},{6,5},{7,6},{8,11},{9,8},{10,9... | collective-permute-start | bytes 1671176 | tf_op jit(solution)/shard_map/ppermute | solution.py:28
  381.2 55.9 %collective-permute-start.39 = (f32[136,128]{1,0:T(8,128)}, f32[136,128]{1,0:T(8,128)}, u32[]{:S(2)}, u32[]{:S(2)}) collective-permute-start(f32[136,128]{1,0:T(8,128)} %fusion.43), channel_id=1, source_target_pairs={{0,16},{4,20},{8,24},{12,28},{16,0},{20,4},{24,8},{28,12},{1,17},{... | collective-permute-start | bytes 208904 | tf_op jit(solution)/shard_map/ppermute | solution.py:83
  387.7 30.6 %collective-permute-start.27 = (bf16[272,1024]{1,0:T(8,128)(2,1)}, bf16[272,1024]{1,0:T(8,128)(2,1)}, u32[]{:S(2)}, u32[]{:S(2)}) collective-permute-start(bf16[272,1024]{1,0:T(8,128)(2,1)} %get-tuple-element.76), channel_id=1, source_target_pairs={{0,1},{1,2},{2,3},{3,0},{4,5},{5,6},{6,7},{7,4},{8,9},{9,10},{10,1... | collective-permute-start | bytes 1671176 | tf_op jit(solution)/shard_map/ppermute | solution.py:24
  390.1 78.8 %collective-permute-start.29 = (bf16[272,1024]{1,0:T(8,128)(2,1)}, bf16[272,1024]{1,0:T(8,128)(2,1)S(1)}, u32[]{:S(2)}, u32[]{:S(2)}) collective-permute-start(bf16[272,1024]{1,0:T(8,128)(2,1)} %copy-done.40), channel_id=1, source_target_pairs={{0,3},{1,0},{2,1},{3,2},{4,7},{5,4},{6,5},{7,6},{8,11},{9,8},{10,9... | collective-permute-start | bytes 1671176 | tf_op jit(solution)/shard_map/ppermute | solution.py:28
  394.0 38.0 %all-to-all-start.4 = ((bf16[4,128,256]{2,1,0:T(8,128)(2,1)}), bf16[4,128,256]{2,1,0:T(8,128)(2,1)S(1)}, u32[]{:S(2)}, u32[]{:S(2)}) async-start(bf16[4,128,256]{2,1,0:T(8,128)(2,1)} %copy.81), calls=%async_computation.4 | async-start | bytes 524288 | tf_op jit(solution)/shard_map/all_to_all | solution.py:790
  420.3 48.7 %collective-permute-start.28 = (bf16[272,1024]{1,0:T(8,128)(2,1)}, bf16[272,1024]{1,0:T(8,128)(2,1)S(1)}, u32[]{:S(2)}, u32[]{:S(2)}) collective-permute-start(bf16[272,1024]{1,0:T(8,128)(2,1)} %add_convert_fusion), channel_id=1, source_target_pairs={{0,1},{1,2},{2,3},{3,0},{4,5},{5,6},{6,7},{7,4},{8,9},{9,10},{10,1... | collective-permute-start | bytes 1671176 | tf_op jit(solution)/shard_map/ppermute | solution.py:24
  432.7 63.2 %all-to-all-start.5 = ((bf16[4,128,2304]{2,1,0:T(8,128)(2,1)}), bf16[4,128,2304]{2,1,0:T(8,128)(2,1)}, u32[]{:S(2)}, u32[]{:S(2)}) async-start(bf16[4,128,2304]{2,1,0:T(8,128)(2,1)} %fusion), calls=%async_computation.5 | async-start | bytes 4718592 | tf_op jit(solution)/shard_map/all_to_all | solution.py:109
  438.2 28.1 %collective-permute-start.40 = (f32[136,128]{1,0:T(8,128)S(1)}, f32[136,128]{1,0:T(8,128)S(1)}, u32[]{:S(2)}, u32[]{:S(2)}) collective-permute-start(f32[136,128]{1,0:T(8,128)S(1)} %fusion.54), channel_id=1, source_target_pairs={{0,8},{4,12},{8,0},{12,4},{16,24},{20,28},{24,16},{28,20},{1,9},{5... | collective-permute-start | bytes 208904 | tf_op jit(solution)/shard_map/ppermute | solution.py:83
  441.5 44.8 %collective-permute-start.22 = (bf16[272,1024]{1,0:T(8,128)(2,1)S(1)}, bf16[272,1024]{1,0:T(8,128)(2,1)S(1)}, u32[]{:S(2)}, u32[]{:S(2)}) collective-permute-start(bf16[272,1024]{1,0:T(8,128)(2,1)S(1)} %add_convert_fusion.2), channel_id=1, source_target_pairs={{0,1},{1,2},{2,3},{3,0},{4,5},{5,6},{6,7},{7,4},{8,9},{9,10},{10,1... | collective-permute-start | bytes 1671176 | tf_op jit(solution)/shard_map/ppermute | solution.py:24
  (99 other events, 1348.6 us)
